TPU v7x, 32 devices: a whole 2x2x4 slice. The times are simulated.
32 devices in a mesh: row: 4 (over y, core), col: 8 (over z, x).
Axes of the slice: x: 2, y: 2, z: 4, core: 2. Of those that a mesh axis runs over, the one named last changes fastest.
Arguments:
- inputs: bfloat16 [1024, 6144], P('col', 'row'), may hold values from -1200 to 1200
- norm_gain: float32 [6144], P('row'), may hold values from 0.5 to 9
- weight_in: bfloat16 [6144, 24576], P('row', 'col'), may hold values from -1 to 1
- weight_out: bfloat16 [24576, 6144], P('col', 'row'), may hold values from -0.0390625 to 0.0390625
- cotangent: bfloat16 [1024, 6144], P('col', 'row'), may hold values from -4 to 4
Outputs:
- branch: bfloat16 [1024, 6144], P('col', 'row')
- input_gradient: bfloat16 [1024, 6144], P('col', 'row')
- in_gradient: float32 [6144, 24576], P('row', 'col')
- out_gradient: float32 [24576, 6144], P('col', 'row')
- gain_gradient: float32 [6144], P('row')
All inputs are finite; a program needn't handle non-finite values.
Results may differ from a plain program's by a relative error of at most 0.039.
Values may be sent and summed in bfloat16 or wider, within the bound.
A program may use at most 128 MiB of HBM per device.

v0:
```python
import jax
import jax.numpy as jnp
from jax import lax
from jax.sharding import PartitionSpec as P

D = 6144


epsilon = 1e-06


def gelu_value(value):
    return jax.nn.gelu(value, approximate=False)


def gelu_slope(value, upstream):
    return jax.vjp(gelu_value, value)[1](upstream)[0]


def per_device(inputs, norm_gain, weight_in, weight_out, cotangent):
    floats = inputs.astype(jnp.float32)
    totals, squares = lax.psum((jnp.sum(floats, axis=1), jnp.sum(floats * floats, axis=1)), "row")
    center = totals / D
    spread = lax.rsqrt(squares / D - center * center + epsilon)
    normed = (floats - center[:, None]) * spread[:, None]
    scaled = (normed * norm_gain[None, :]).astype(jnp.bfloat16)
    normed_all = lax.all_gather(scaled, "col", axis=0, tiled=True)
    hidden_part = lax.psum_scatter(
        jnp.dot(normed_all, weight_in, preferred_element_type=jnp.float32).astype(jnp.bfloat16),
        "row",
        scatter_dimension=0,
        tiled=True,
    ).astype(jnp.float32)
    active_part = gelu_value(hidden_part).astype(jnp.bfloat16)
    active_all = lax.all_gather(active_part, "row", axis=0, tiled=True)
    branch = lax.psum_scatter(
        jnp.dot(active_all, weight_out, preferred_element_type=jnp.float32).astype(jnp.bfloat16),
        "col",
        scatter_dimension=0,
        tiled=True,
    )
    cotangent_all = lax.all_gather(cotangent, "col", axis=0, tiled=True)
    active_part_gradient = lax.psum_scatter(
        lax.dot_general(
            cotangent_all, weight_out, (((1,), (1,)), ((), ())), preferred_element_type=jnp.float32
        ).astype(jnp.bfloat16),
        "row",
        scatter_dimension=0,
        tiled=True,
    ).astype(jnp.float32)
    slope_part = gelu_slope(hidden_part, active_part_gradient).astype(jnp.bfloat16)
    slope_all = lax.all_gather(slope_part, "row", axis=0, tiled=True)
    out_gradient = lax.dot_general(
        active_all, cotangent_all, (((0,), (0,)), ((), ())), preferred_element_type=jnp.float32
    )
    in_gradient = lax.dot_general(
        normed_all, slope_all, (((0,), (0,)), ((), ())), preferred_element_type=jnp.float32
    )
    normed_gradient = lax.psum_scatter(
        lax.dot_general(
            slope_all, weight_in, (((1,), (1,)), ((), ())), preferred_element_type=jnp.float32
        ).astype(jnp.bfloat16),
        "col",
        scatter_dimension=0,
        tiled=True,
    ).astype(jnp.float32)
    gain_gradient = lax.psum(jnp.sum(normed_gradient * normed, axis=0), "col")
    scaled_gradient = normed_gradient * norm_gain[None, :]
    mean_gradient, mean_cross = lax.psum(
        (jnp.sum(scaled_gradient, axis=1), jnp.sum(scaled_gradient * normed, axis=1)), "row"
    )
    input_gradient = spread[:, None] * (
        scaled_gradient - mean_gradient[:, None] / D - normed * mean_cross[:, None] / D
    )
    return (branch, input_gradient.astype(jnp.bfloat16), in_gradient, out_gradient, gain_gradient)


def solution(mesh):
    in_specs = (P("col", "row"), P("row"), P("row", "col"), P("col", "row"), P("col", "row"))
    out_specs = (P("col", "row"), P("col", "row"), P("row", "col"), P("col", "row"), P("row"))
    return jax.shard_map(
        per_device, mesh=mesh, in_specs=in_specs, out_specs=out_specs, check_vma=False
    )
```

profile of v0, /device:TPU:0, one launch (start us, length us, event | category | flops | bytes accessed | tf_op | source)
XLA Modules:
  0.0 530.2 jit_solution(16146614391540827615)
XLA Ops:
  7.2 1.2 convert_reduce_fusion
  8.4 8.4 %all-reduce.1 = (f32[128]{0:T(128)S(1)}, f32[128]{0:T(128)S(1)}) all-reduce(f32[128]{0:T(128)S(1)} %get-tuple-element.9, f32[128]{0:T(128)S(1)} %get-tuple-element.8), channel_id=1, replica_groups=mesh['row'=4,'col'=8] {'row'}, use_global_device_ids=true, to_apply=%region_3.0 | all-reduce | flops 256 | bytes 2048 | tf_op jit(solution)/shard_map/psum | solution.py:22
  16.8 2.0 fusion.49
  19.6 60.1 %all-gather.5.cloned.1.call-done = bf16[1024,1536]{1,0:T(8,128)(2,1)} async-done(((bf16[128,1536]{1,0:T(8,128)(2,1)}), bf16[1024,1536]{1,0:T(8,128)(2,1)}) %all-gather.5.cloned.1.call-update) | async-done | bytes 3145744 | tf_op jit(solution)/shard_map/all_gather | solution.py:27
  79.7 15.1 %convolution_convert_fusion.1 = bf16[1024,3072]{1,0:T(8,128)(2,1)} fusion(bf16[1024,1536]{1,0:T(8,128)(2,1)} %all-gather.5.cloned.1.call-done, bf16[1536,3072]{1,0:T(8,128)(2,1)} %param.7), kind=kOutput, calls=%fused_computation.1 | convolution fusion | flops 9666822144 | bytes 18874368 | tf_op jit(solution)/shard_map/dot_general | solution.py:29
  94.9 46.2 %all-gather.9.cloned.1.call-done = bf16[1024,1536]{1,0:T(8,128)(2,1)} async-done(((bf16[128,1536]{1,0:T(8,128)(2,1)}), bf16[1024,1536]{1,0:T(8,128)(2,1)}) %all-gather.9.cloned.1.call-update) | async-done | bytes 3145744 | tf_op jit(solution)/shard_map/all_gather | solution.py:42
  141.0 15.1 %convolution_convert_fusion = bf16[1024,3072]{1,0:T(8,128)(2,1)} fusion(bf16[1024,1536]{1,0:T(8,128)(2,1)} %all-gather.9.cloned.1.call-done, bf16[3072,1536]{1,0:T(8,128)(2,1)} %param.8), kind=kOutput, calls=%fused_computation | convolution fusion | flops 9666822144 | bytes 18874368 | tf_op jit(solution)/shard_map/dot_general | solution.py:44
  156.2 44.9 %reduce-scatter.5.cloned.1.call-done = bf16[256,3072]{1,0:T(8,128)(2,1)} async-done(((bf16[1024,3072]{1,0:T(8,128)(2,1)}), bf16[256,3072]{1,0:T(8,128)(2,1)}) %reduce-scatter.5.cloned.1.call-update) | async-done | bytes 1572880 | tf_op jit(solution)/shard_map/reduce_scatter | solution.py:28
  201.2 61.5 %reduce-scatter.9.cloned.1.call-done = bf16[256,3072]{1,0:T(8,128)(2,1)} async-done(((bf16[1024,3072]{1,0:T(8,128)(2,1)}), bf16[256,3072]{1,0:T(8,128)(2,1)}) %reduce-scatter.9.cloned.1.call-update) | async-done | bytes 1572880 | tf_op jit(solution)/shard_map/reduce_scatter | solution.py:43
  262.7 9.4 %fusion.36 = (bf16[256,3072]{1,0:T(8,128)(2,1)}, f32[256,3072]{1,0:T(8,128)S(1)}) fusion(bf16[256,3072]{1,0:T(8,128)(2,1)} %reduce-scatter.9.cloned.1.call-done, bf16[256,3072]{1,0:T(8,128)(2,1)} %reduce-scatter.5.cloned.1.call-done), kind=kLoop, calls=%fused_computation.45 | loop fusion | flops 58195968 | bytes 7864320 | tf_op jit(solution)/shard_map/convert_element_type | solution.py:51
  272.1 3.1 fusion.1
  275.5 43.2 %all-gather.11.cloned.1.call-done = bf16[1024,3072]{1,0:T(8,128)(2,1)} async-done(((bf16[256,3072]{1,0:T(8,128)(2,1)}), bf16[1024,3072]{1,0:T(8,128)(2,1)}) %all-gather.11.cloned.1.call-update) | async-done | bytes 6291472 | tf_op jit(solution)/shard_map/all_gather | solution.py:52
  318.6 15.5 %convolution_convert_fusion.2 = bf16[1024,1536]{1,0:T(8,128)(2,1)} fusion(bf16[1024,3072]{1,0:T(8,128)(2,1)} %all-gather.11.cloned.1.call-done, bf16[1536,3072]{1,0:T(8,128)(2,1)} %param.7), kind=kOutput, calls=%fused_computation.7 | convolution fusion | flops 9665249280 | bytes 18874368 | tf_op jit(solution)/shard_map/dot_general | solution.py:60
  334.2 32.8 %all-gather.7.cloned.1.call-done = bf16[1024,3072]{1,0:T(8,128)(2,1)} async-done(((bf16[256,3072]{1,0:T(8,128)(2,1)}), bf16[1024,3072]{1,0:T(8,128)(2,1)}) %all-gather.7.cloned.1.call-update) | async-done | bytes 6291472 | tf_op jit(solution)/shard_map/all_gather | solution.py:35
  367.0 15.6 %convolution_convert_fusion.3 = bf16[1024,1536]{1,0:T(8,128)(2,1)} fusion(bf16[1024,3072]{1,0:T(8,128)(2,1)} %all-gather.7.cloned.1.call-done, bf16[3072,1536]{1,0:T(8,128)(2,1)} %param.8), kind=kOutput, calls=%fused_computation.8 | convolution fusion | flops 9665249280 | bytes 18874368 | tf_op jit(solution)/shard_map/dot_general | solution.py:37
  382.7 1.9 copy-done.3
  384.6 16.0 %fusion.54 = f32[3072,1536]{1,0:T(8,128)} fusion(bf16[1024,3072]{1,0:T(8,128)(2,1)} %all-gather.7.cloned.1.call-done, bf16[1024,1536]{1,0:T(8,128)(2,1)S(1)} %copy-done.3), kind=kOutput, calls=%fused_computation.70 | convolution fusion | flops 9663676416 | bytes 28311552 | tf_op jit(solution)/shard_map/dot_general | solution.py:53
  400.6 16.1 %fusion.53 = f32[1536,3072]{1,0:T(8,128)} fusion(bf16[1024,1536]{1,0:T(8,128)(2,1)S(1)} %copy-done.2, bf16[1024,3072]{1,0:T(8,128)(2,1)} %all-gather.11.cloned.1.call-done), kind=kOutput, calls=%fused_computation.69 | convolution fusion | flops 9663676416 | bytes 28311552 | tf_op jit(solution)/shard_map/dot_general | solution.py:56
  416.8 28.3 %reduce-scatter.11.cloned.1.call-done = bf16[128,1536]{1,0:T(8,128)(2,1)} async-done(((bf16[1024,1536]{1,0:T(8,128)(2,1)}), bf16[128,1536]{1,0:T(8,128)(2,1)}) %reduce-scatter.11.cloned.1.call-update) | async-done | bytes 393232 | tf_op jit(solution)/shard_map/reduce_scatter | solution.py:59
  445.1 1.4 fusion.45
  446.4 5.9 %all-reduce = (f32[128]{0:T(128)S(1)}, f32[128]{0:T(128)S(1)}) all-reduce(f32[128]{0:T(128)S(1)} %get-tuple-element.6, f32[128]{0:T(128)S(1)} %get-tuple-element.7), channel_id=1, replica_groups=mesh['row'=4,'col'=8] {'row'}, use_global_device_ids=true, to_apply=%region_11.0 | all-reduce | flops 256 | bytes 2048 | tf_op jit(solution)/shard_map/psum | solution.py:69
  452.3 21.5 %psum.39 = f32[1536]{0:T(1024)} all-reduce(f32[1536]{0:T(1024)S(1)} %get-tuple-element.5), channel_id=1, replica_groups=mesh['row'=4,'col'=8] {'col'}, use_global_device_ids=true, to_apply=%region_13.0 | all-reduce | flops 1536 | bytes 12288 | tf_op jit(solution)/shard_map/psum | solution.py:67
  473.9 2.1 fusion.43
  476.0 47.4 %reduce-scatter.7.cloned.1.call-done = bf16[128,1536]{1,0:T(8,128)(2,1)} async-done(((bf16[1024,1536]{1,0:T(8,128)(2,1)}), bf16[128,1536]{1,0:T(8,128)(2,1)}) %reduce-scatter.7.cloned.1.call-update) | async-done | bytes 393232 | tf_op jit(solution)/shard_map/reduce_scatter | solution.py:36
  (25 shorter events, 1.3 us)
Async XLA Ops:
  7.2 72.6 %all-gather.5.cloned.1.call-start = ((), (), s32[]{:S(2)}) async-start(), calls=%async_computation.4 | async-start | bytes 3538944 | tf_op jit(solution)/shard_map/all_gather | solution.py:27
  18.8 122.2 %all-gather.9.cloned.1.call-start = ((), (), s32[]{:S(2)}) async-start(), calls=%async_computation.8 | async-start | bytes 3538944 | tf_op jit(solution)/shard_map/all_gather | solution.py:42
  19.6 181.6 %reduce-scatter.5.cloned.1.call-start = ((), (), s32[]{:S(2)}) async-start(), calls=%async_computation.5 | async-start | bytes 7864320 | tf_op jit(solution)/shard_map/reduce_scatter | solution.py:28
  94.8 167.9 %reduce-scatter.9.cloned.1.call-start = ((), (), s32[]{:S(2)}) async-start(), calls=%async_computation.9 | async-start | bytes 7864320 | tf_op jit(solution)/shard_map/reduce_scatter | solution.py:43
  156.2 162.5 %all-gather.11.cloned.1.call-start = ((), (), s32[]{:S(2)}) async-start(), calls=%async_computation.10 | async-start | bytes 7864320 | tf_op jit(solution)/shard_map/all_gather | solution.py:52
  272.1 95.0 %all-gather.7.cloned.1.call-start = ((), (), s32[]{:S(2)}) async-start(), calls=%async_computation.6 | async-start | bytes 7864320 | tf_op jit(solution)/shard_map/all_gather | solution.py:35
  275.2 169.8 %reduce-scatter.11.cloned.1.call-start = ((), (), s32[]{:S(2)}) async-start(), calls=%async_computation.11 | async-start | bytes 3538944 | tf_op jit(solution)/shard_map/reduce_scatter | solution.py:59
  334.2 189.2 %reduce-scatter.7.cloned.1.call-start = ((), (), s32[]{:S(2)}) async-start(), calls=%async_computation.7 | async-start | bytes 3538944 | tf_op jit(solution)/shard_map/reduce_scatter | solution.py:36
  382.6 1.9 copy-start.3
  384.6 16.0 %copy-start.2 = (bf16[1024,1536]{1,0:T(8,128)(2,1)S(1)}, bf16[1024,1536]{1,0:T(8,128)(2,1)}, u32[]{:S(2)}) copy-start(bf16[1024,1536]{1,0:T(8,128)(2,1)} %all-gather.5.cloned.1.call-done) | copy-start | bytes 9437188
  400.6 44.4 %copy-start = (bf16[128,1536]{1,0:T(8,128)(2,1)S(1)}, bf16[128,1536]{1,0:T(8,128)(2,1)}, u32[]{:S(2)}) copy-start(bf16[128,1536]{1,0:T(8,128)(2,1)} %param.5) | copy-start | bytes 1179652
  400.6 44.4 %copy-start.1 = (f32[1536]{0:T(1024)S(1)}, f32[1536]{0:T(1024)}, u32[]{:S(2)}) copy-start(f32[1536]{0:T(1024)} %param.6) | copy-start | bytes 18436
Sparse Core Ops, SparseCore 0:
  18.9 60.7 all-gather.4
  81.9 59.0 all-gather.8
  144.1 56.9 reduce-scatter.4
  204.3 58.3 reduce-scatter.8
  272.2 46.3 all-gather.10
  320.6 46.3 all-gather.6
  370.6 74.3 reduce-scatter.10
  449.2 74.1 reduce-scatter.6
where the time goes:
time: 531 us; the launch traced here: 530 us
  waiting for transfers between devices  365 us (69%)
  matrix products  93.5 us (18%)
  blocking collectives  35.8 us (7%)
  other arithmetic  19.2 us (4%)
  between operations  14.2 us (3%)
    reduce_scatter x1, waiting for transfers between devices, per_device(): lax.psum_scatter(lax.dot_general(cotangent_all, weight_out, (((1,), (1,))...  61.5 us
    all_gather x1, waiting for transfers between devices, per_device(): normed_all = lax.all_gather(scaled, 'col', axis=0, tiled=True)  60.1 us
    reduce_scatter x1, waiting for transfers between devices, per_device(): lax.psum_scatter(jnp.dot(active_all, weight_out, preferred_element_type=j...  47.4 us
    all_gather x1, waiting for transfers between devices, per_device(): cotangent_all = lax.all_gather(cotangent, 'col', axis=0, tiled=True)  46.2 us
    reduce_scatter x1, waiting for transfers between devices, per_device(): lax.psum_scatter(jnp.dot(normed_all, weight_in, preferred_element_type=jn...  44.9 us
    all_gather x1, waiting for transfers between devices, per_device(): slope_all = lax.all_gather(slope_part, 'row', axis=0, tiled=True)  43.2 us
    all_gather x1, waiting for transfers between devices, per_device(): active_all = lax.all_gather(active_part, 'row', axis=0, tiled=True)  32.8 us
    reduce_scatter x1, waiting for transfers between devices, per_device(): lax.psum_scatter(lax.dot_general(slope_all, weight_in, (((1,), (1,)), (()...  28.3 us
  transfers between devices with their start and end apart: 8, of which 8 were waited for; matrix products, arithmetic and copies ran while one was open for 19% of the time, Pallas kernels for 0%

commit v1 on v0

v1 whole, which is shorter than its diff:
```python
import jax
import jax.numpy as jnp
from jax import lax
from jax.sharding import PartitionSpec as P

epsilon = 1e-06


def gelu_value(value):
    return jax.nn.gelu(value, approximate=False)


def gelu_slope(value, upstream):
    return jax.vjp(gelu_value, value)[1](upstream)[0]


def shifted(value, axis, outer, inner, outer_step, inner_step):
    pairs = []
    for first in range(outer):
        for second in range(inner):
            source = ((first + outer_step) % outer) * inner + (second + inner_step) % inner
            pairs.append((source, first * inner + second))
    return lax.ppermute(value, axis, pairs)


def make_per_device(rows, cols):
    core_n = 2
    y_n = rows // core_n
    z_n = 4 if cols % 4 == 0 else 1
    x_n = cols // z_n

    def along_z(value, step):
        return value if step % z_n == 0 else shifted(value, "col", z_n, x_n, step, 0)

    def along_x(value, step):
        return value if step % x_n == 0 else shifted(value, "col", z_n, x_n, 0, step)

    def along_y(value, step):
        return value if step % y_n == 0 else shifted(value, "row", y_n, core_n, step, 0)

    def along_core(value, step):
        return value if step % core_n == 0 else shifted(value, "row", y_n, core_n, 0, step)

    def gather_col(block):
        chunks = []
        for dz in range(z_n):
            piece = along_z(block, dz)
            chunks.append(jnp.concatenate([along_x(piece, dx) for dx in range(x_n)], axis=0))
        return chunks

    def send_col(partial, dz):
        blocks = jnp.split(partial, x_n, axis=0)
        total = sum(along_x(blocks[dx], -dx).astype(jnp.float32) for dx in range(x_n))
        return along_z(total.astype(jnp.bfloat16), -dz).astype(jnp.float32)

    def scatter_row(partial):
        place = lax.axis_index("row")
        y, core = place // core_n, place % core_n
        half = partial.shape[0] // core_n
        total = 0.0
        for step in range(core_n):
            part = lax.dynamic_slice_in_dim(partial, ((core + step) % core_n) * half, half, 0)
            total = total + along_core(part, -step).astype(jnp.float32)
        total = total.astype(jnp.bfloat16)
        quarter = half // y_n
        result = 0.0
        for step in range(y_n):
            part = lax.dynamic_slice_in_dim(total, ((y + step) % y_n) * quarter, quarter, 0)
            result = result + along_y(part, -step).astype(jnp.float32)
        return result

    def gather_row(part):
        place = lax.axis_index("row")
        y, core = place // core_n, place % core_n
        pieces = [along_y(part, step) for step in range(y_n)]
        half = jnp.concatenate([lax.select_n((k - y) % y_n, *pieces) if y_n > 1 else part for k in range(y_n)], axis=0)
        pieces = [along_core(half, step) for step in range(core_n)]
        return jnp.concatenate([lax.select_n((k - core) % core_n, *pieces) for k in range(core_n)], axis=0)

    def per_device(inputs, norm_gain, weight_in, weight_out, cotangent):
        width = inputs.shape[1] * rows
        floats = inputs.astype(jnp.float32)
        stats = lax.psum(jnp.stack([jnp.sum(floats, axis=1), jnp.sum(floats * floats, axis=1)]), "row")
        center = stats[0] / width
        spread = lax.rsqrt(stats[1] / width - center * center + epsilon)
        normed = (floats - center[:, None]) * spread[:, None]
        scaled = (normed * norm_gain[None, :]).astype(jnp.bfloat16)

        cot_chunks = gather_col(cotangent)
        scaled_chunks = gather_col(scaled)
        back = [
            scatter_row(
                lax.dot_general(c, weight_out, (((1,), (1,)), ((), ())), preferred_element_type=jnp.float32).astype(jnp.bfloat16)
            )
            for c in cot_chunks
        ]
        hidden = [
            scatter_row(jnp.dot(s, weight_in, preferred_element_type=jnp.float32).astype(jnp.bfloat16)) for s in scaled_chunks
        ]
        active = [gather_row(gelu_value(h).astype(jnp.bfloat16)) for h in hidden]
        slope = [gather_row(gelu_slope(h, b).astype(jnp.bfloat16)) for h, b in zip(hidden, back)]

        branch = 0.0
        for dz in range(z_n):
            branch = branch + send_col(
                jnp.dot(active[dz], weight_out, preferred_element_type=jnp.float32).astype(jnp.bfloat16), dz
            )
        normed_gradient = 0.0
        for dz in range(z_n):
            normed_gradient = normed_gradient + send_col(
                lax.dot_general(
                    slope[dz], weight_in, (((1,), (1,)), ((), ())), preferred_element_type=jnp.float32
                ).astype(jnp.bfloat16),
                dz,
            )
        out_gradient = lax.dot_general(
            jnp.concatenate(active), jnp.concatenate(cot_chunks), (((0,), (0,)), ((), ())), preferred_element_type=jnp.float32
        )
        in_gradient = lax.dot_general(
            jnp.concatenate(scaled_chunks), jnp.concatenate(slope), (((0,), (0,)), ((), ())), preferred_element_type=jnp.float32
        )
        gain_gradient = lax.psum(jnp.sum(normed_gradient * normed, axis=0), "col")
        scaled_gradient = normed_gradient * norm_gain[None, :]
        sums = lax.psum(jnp.stack([jnp.sum(scaled_gradient, axis=1), jnp.sum(scaled_gradient * normed, axis=1)]), "row") / width
        input_gradient = spread[:, None] * (scaled_gradient - sums[0][:, None] - normed * sums[1][:, None])
        return (
            branch.astype(jnp.bfloat16),
            input_gradient.astype(jnp.bfloat16),
            in_gradient,
            out_gradient,
            gain_gradient,
        )

    return per_device


def solution(mesh):
    in_specs = (P("col", "row"), P("row"), P("row", "col"), P("col", "row"), P("col", "row"))
    out_specs = (P("col", "row"), P("col", "row"), P("row", "col"), P("col", "row"), P("row"))
    per_device = make_per_device(mesh.shape["row"], mesh.shape["col"])
    return jax.shard_map(per_device, mesh=mesh, in_specs=in_specs, out_specs=out_specs, check_vma=False)
```

time: 531 us -> 480 us (0.904); the launches traced: 530 us -> 472 us
  waiting for transfers between devices: 365 us -> 199 us
  starting transfers between devices: 0.51 us -> 65.2 us
  matrix products: 93.5 us -> 121 us
  other arithmetic: 19.2 us -> 35.2 us
  between operations: 14.2 us -> 2.06 us
  local copies, waits for them, and re-layouts: 1.9 us -> 13.6 us
    ppermute x0 -> x60, waiting for transfers between devices: none -> 199 us  [shifted(): return lax.ppermute(value, axis, pairs)]
    all_gather x4 -> x0, waiting for transfers between devices: 182 us -> none  [the longest x1 60.1 us: per_device(): normed_all = lax.all_gather(scaled, 'col', axis=0, tiled=True)]
    reduce_scatter x4 -> x0, waiting for transfers between devices: 182 us -> none  [the longest x1 61.5 us: per_device(): lax.psum_scatter(lax.dot_general(cotangent_all, weight_out, (((1,), (1,))...]
    ppermute x0 -> x60, starting transfers between devices: none -> 65.2 us  [shifted(): return lax.ppermute(value, axis, pairs)]
    dot_general x6 -> x18, matrix products: 93.5 us -> 121 us  [the longest x4 25.5 us: per_device(): lax.dot_general(slope[dz], weight_in, (((1,), (1,)), ((), ())), preferred...]
    unnamed x0 -> x17, other arithmetic: none -> 14.1 us
    unnamed x8 -> x45, local copies, waits for them, and re-layouts: 1.9 us -> 10.4 us
    convert_element_type x3 -> x23, other arithmetic: 14.5 us -> 14.1 us  [the longest x4 8.08 us: per_device(): gelu_slope(h, b).astype(jnp.bfloat16)]
  transfers between devices with their start and end apart: 8 -> 60, of which waited for: 8 -> 24; matrix products, arithmetic and copies ran while one was open for 19% -> 36% of each run, Pallas kernels for 0% -> 0%
where the time goes in v1:
time: 480 us; the launch traced here: 472 us
  waiting for transfers between devices  199 us (41%)
  matrix products  121 us (25%)
  starting transfers between devices  65.2 us (14%)
  blocking collectives  35.9 us (7%)
  other arithmetic  35.2 us (7%)
  local copies, waits for them, and re-layouts  13.6 us (3%)
    ppermute x60, waiting for transfers between devices, shifted(): return lax.ppermute(value, axis, pairs)  199 us
    ppermute x60, starting transfers between devices, shifted(): return lax.ppermute(value, axis, pairs)  65.2 us
    dot_general x4, matrix products, per_device(): lax.dot_general(slope[dz], weight_in, (((1,), (1,)), ((), ())), preferred...  25.5 us
    dot_general x4, matrix products, per_device(): lax.dot_general(c, weight_out, (((1,), (1,)), ((), ())), preferred_elemen...  25.4 us
    psum x1, blocking collectives, per_device(): gain_gradient = lax.psum(jnp.sum(normed_gradient * normed, axis=0), 'col')  24.3 us
    dot_general x4, matrix products, per_device(): jnp.dot(active[dz], weight_out, preferred_element_type=jnp.float32)  21.6 us
    dot_general x4, matrix products, per_device(): jnp.dot(s, weight_in, preferred_element_type=jnp.float32)  18.3 us
    dot_general x1, matrix products, per_device(): lax.dot_general(jnp.concatenate(scaled_chunks), jnp.concatenate(slope), (...  16.8 us
  transfers between devices with their start and end apart: 60, of which 24 were waited for; matrix products, arithmetic and copies ran while one was open for 36% of the time, Pallas kernels for 0%

profile of v1, /device:TPU:0, one launch (start us, length us, event | category | flops | bytes accessed | tf_op | source)
XLA Modules:
  0.0 471.7 jit_solution(1496929430980374664)
XLA Ops:
  20.6 6.5 %convolution_convert_fusion.3 = bf16[256,3072]{1,0:T(8,128)(2,1)S(1)} fusion(bf16[3072,1536]{1,0:T(8,128)(2,1)} %param.8, bf16[128,1536]{1,0:T(8,128)(2,1)S(1)} %collective-permute-done.30, bf16[128,1536]{1,0:T(8,128)(2,1)} %param.9), kind=kOutput, calls=%fused_computation.3 | convolution fusion | flops 2418278400 | bytes 11796480 | tf_op jit(solution)/shard_map/dot_general | solution.py:93
  40.8 32.3 %collective-permute-done.6 = bf16[128,1536]{1,0:T(8,128)(2,1)S(1)} collective-permute-done((bf16[128,1536]{1,0:T(8,128)(2,1)S(1)}, bf16[128,1536]{1,0:T(8,128)(2,1)S(1)}, u32[]{:S(2)}, u32[]{:S(2)}) %collective-permute-start.6) | collective-permute-done | bytes 393248 | tf_op jit(solution)/shard_map/ppermute | solution.py:23
  75.2 8.9 %collective-permute-done.53 = bf16[128,1536]{1,0:T(8,128)(2,1)S(1)} collective-permute-done((bf16[128,1536]{1,0:T(8,128)(2,1)S(1)}, bf16[128,1536]{1,0:T(8,128)(2,1)S(1)}, u32[]{:S(2)}, u32[]{:S(2)}) %collective-permute-start.53) | collective-permute-done | bytes 393248 | tf_op jit(solution)/shard_map/ppermute | solution.py:23
  115.6 6.4 %convolution_convert_fusion.6 = bf16[256,3072]{1,0:T(8,128)(2,1)S(1)} fusion(bf16[1536,3072]{1,0:T(8,128)(2,1)} %param.7, bf16[128,1536]{1,0:T(8,128)(2,1)S(1)} %collective-permute-done.7, bf16[128,1536]{1,0:T(8,128)(2,1)S(1)} %collective-permute-done.6), kind=kOutput, calls=%fused_computation.6 | convolution fusion | flops 2418278400 | bytes 11796480 | tf_op jit(solution)/shard_map/dot_general | solution.py:98
  144.2 6.7 %collective-permute-done.32 = bf16[64,3072]{1,0:T(8,128)(2,1)S(1)} collective-permute-done((bf16[64,3072]{1,0:T(8,128)(2,1)S(1)}, bf16[64,3072]{1,0:T(8,128)(2,1)S(1)}, u32[]{:S(2)}, u32[]{:S(2)}) %collective-permute-start.32) | collective-permute-done | bytes 393248 | tf_op jit(solution)/shard_map/ppermute | solution.py:23
  151.8 7.5 %collective-permute-done.2 = bf16[64,3072]{1,0:T(8,128)(2,1)S(1)} collective-permute-done((bf16[64,3072]{1,0:T(8,128)(2,1)S(1)}, bf16[64,3072]{1,0:T(8,128)(2,1)S(1)}, u32[]{:S(2)}, u32[]{:S(2)}) %collective-permute-start.2) | collective-permute-done | bytes 393248 | tf_op jit(solution)/shard_map/ppermute | solution.py:23
  168.7 24.4 %collective-permute-done.25 = bf16[64,3072]{1,0:T(8,128)(2,1)S(1)} collective-permute-done((bf16[64,3072]{1,0:T(8,128)(2,1)S(1)}, bf16[64,3072]{1,0:T(8,128)(2,1)S(1)}, u32[]{:S(2)}, u32[]{:S(2)}) %collective-permute-start.25) | collective-permute-done | bytes 393248 | tf_op jit(solution)/shard_map/ppermute | solution.py:23
  219.3 7.4 %collective-permute-done.33 = bf16[64,3072]{1,0:T(8,128)(2,1)S(1)} collective-permute-done((bf16[64,3072]{1,0:T(8,128)(2,1)S(1)}, bf16[64,3072]{1,0:T(8,128)(2,1)S(1)}, u32[]{:S(2)}, u32[]{:S(2)}) %collective-permute-start.33) | collective-permute-done | bytes 393248 | tf_op jit(solution)/shard_map/ppermute | solution.py:23
  227.8 7.3 %collective-permute-done.26 = bf16[64,3072]{1,0:T(8,128)(2,1)S(1)} collective-permute-done((bf16[64,3072]{1,0:T(8,128)(2,1)S(1)}, bf16[64,3072]{1,0:T(8,128)(2,1)S(1)}, u32[]{:S(2)}, u32[]{:S(2)}) %collective-permute-start.26) | collective-permute-done | bytes 393248 | tf_op jit(solution)/shard_map/ppermute | solution.py:23
  236.2 7.4 %collective-permute-done.56 = bf16[64,3072]{1,0:T(8,128)(2,1)S(1)} collective-permute-done((bf16[64,3072]{1,0:T(8,128)(2,1)S(1)}, bf16[64,3072]{1,0:T(8,128)(2,1)S(1)}, u32[]{:S(2)}, u32[]{:S(2)}) %collective-permute-start.56) | collective-permute-done | bytes 393248 | tf_op jit(solution)/shard_map/ppermute | solution.py:23
  243.7 8.4 %collective-permute-done.18 = bf16[64,3072]{1,0:T(8,128)(2,1)S(1)} collective-permute-done((bf16[64,3072]{1,0:T(8,128)(2,1)S(1)}, bf16[64,3072]{1,0:T(8,128)(2,1)S(1)}, u32[]{:S(2)}, u32[]{:S(2)}) %collective-permute-start.18) | collective-permute-done | bytes 393248 | tf_op jit(solution)/shard_map/ppermute | solution.py:23
  252.2 8.3 %collective-permute-done.48 = bf16[64,3072]{1,0:T(8,128)(2,1)S(1)} collective-permute-done((bf16[64,3072]{1,0:T(8,128)(2,1)S(1)}, bf16[64,3072]{1,0:T(8,128)(2,1)S(1)}, u32[]{:S(2)}, u32[]{:S(2)}) %collective-permute-start.48) | collective-permute-done | bytes 393248 | tf_op jit(solution)/shard_map/ppermute | solution.py:23
  260.6 8.3 %collective-permute-done.10 = bf16[64,3072]{1,0:T(8,128)(2,1)S(1)} collective-permute-done((bf16[64,3072]{1,0:T(8,128)(2,1)S(1)}, bf16[64,3072]{1,0:T(8,128)(2,1)S(1)}, u32[]{:S(2)}, u32[]{:S(2)}) %collective-permute-start.10) | collective-permute-done | bytes 393248 | tf_op jit(solution)/shard_map/ppermute | solution.py:23
  269.0 7.9 %collective-permute-done.40 = bf16[64,3072]{1,0:T(8,128)(2,1)S(1)} collective-permute-done((bf16[64,3072]{1,0:T(8,128)(2,1)S(1)}, bf16[64,3072]{1,0:T(8,128)(2,1)S(1)}, u32[]{:S(2)}, u32[]{:S(2)}) %collective-permute-start.40) | collective-permute-done | bytes 393248 | tf_op jit(solution)/shard_map/ppermute | solution.py:23
  306.8 6.5 %convolution_convert_fusion.9 = bf16[256,1536]{1,0:T(8,128)(2,1)S(1)} fusion(bf16[1536,3072]{1,0:T(8,128)(2,1)} %param.7, bf16[128,3072]{1,0:T(8,128)(2,1)S(1)} %get-tuple-element.31, bf16[128,3072]{1,0:T(8,128)(2,1)S(1)} %get-tuple-element.33), kind=kOutput, calls=%fused_computation.9 | convolution fusion | flops 2419458048 | bytes 11796480 | tf_op jit(solution)/shard_map/dot_general | solution.py:111
  317.1 6.3 %convolution_convert_fusion.8 = bf16[256,1536]{1,0:T(8,128)(2,1)S(1)} fusion(bf16[1536,3072]{1,0:T(8,128)(2,1)} %param.7, bf16[128,3072]{1,0:T(8,128)(2,1)S(1)} %get-tuple-element.27, bf16[128,3072]{1,0:T(8,128)(2,1)S(1)} %get-tuple-element.29), kind=kOutput, calls=%fused_computation.8 | convolution fusion | flops 2419458048 | bytes 11796480 | tf_op jit(solution)/shard_map/dot_general | solution.py:111
  326.2 6.4 %convolution_convert_fusion.14 = bf16[256,1536]{1,0:T(8,128)(2,1)S(1)} fusion(bf16[3072,1536]{1,0:T(8,128)(2,1)} %param.8, bf16[128,3072]{1,0:T(8,128)(2,1)S(1)} %get-tuple-element.19, bf16[128,3072]{1,0:T(8,128)(2,1)S(1)} %get-tuple-element.21), kind=kOutput, calls=%fused_computation.14 | convolution fusion | flops 2419458048 | bytes 11796480 | tf_op jit(solution)/shard_map/dot_general | solution.py:106
  340.0 13.5 %fusion.112 = f32[3072,1536]{1,0:T(8,128)} fusion(bf16[1024,3072]{1,0:T(8,128)(2,1)S(1)} %get-tuple-element.10, bf16[1024,1536]{1,0:T(8,128)(2,1)S(1)} %copy-done.3), kind=kOutput, calls=%fused_computation.288 | convolution fusion | flops 9663676416 | bytes 28311552 | tf_op jit(solution)/shard_map/dot_general | solution.py:116
  353.5 16.8 %fusion.111 = f32[1536,3072]{1,0:T(8,128)} fusion(bf16[1024,1536]{1,0:T(8,128)(2,1)} %constant_dynamic-update-slice_fusion, bf16[1024,3072]{1,0:T(8,128)(2,1)} %get-tuple-element.26), kind=kOutput, calls=%fused_computation.287 | convolution fusion | flops 9663676416 | bytes 28311552 | tf_op jit(solution)/shard_map/dot_general | solution.py:119
  380.8 8.0 %collective-permute-done.12 = bf16[128,1536]{1,0:T(8,128)(2,1)S(1)} collective-permute-done((bf16[128,1536]{1,0:T(8,128)(2,1)S(1)}, bf16[128,1536]{1,0:T(8,128)(2,1)S(1)}, u32[]{:S(2)}, u32[]{:S(2)}) %collective-permute-start.12) | collective-permute-done | bytes 393248 | tf_op jit(solution)/shard_map/ppermute | solution.py:23
  389.7 7.6 %collective-permute-done.20 = bf16[128,1536]{1,0:T(8,128)(2,1)S(1)} collective-permute-done((bf16[128,1536]{1,0:T(8,128)(2,1)S(1)}, bf16[128,1536]{1,0:T(8,128)(2,1)S(1)}, u32[]{:S(2)}, u32[]{:S(2)}) %collective-permute-start.20) | collective-permute-done | bytes 393248 | tf_op jit(solution)/shard_map/ppermute | solution.py:23
  406.2 12.1 %collective-permute-done.51 = bf16[128,1536]{1,0:T(8,128)(2,1)S(1)} collective-permute-done((bf16[128,1536]{1,0:T(8,128)(2,1)S(1)}, bf16[128,1536]{1,0:T(8,128)(2,1)S(1)}, u32[]{:S(2)}, u32[]{:S(2)}) %collective-permute-start.51) | collective-permute-done | bytes 393248 | tf_op jit(solution)/shard_map/ppermute | solution.py:23
  418.4 18.3 %collective-permute-start.29 = (bf16[128,1536]{1,0:T(8,128)(2,1)}, bf16[128,1536]{1,0:T(8,128)(2,1)S(1)}, u32[]{:S(2)}, u32[]{:S(2)}) collective-permute-start(bf16[128,1536]{1,0:T(8,128)(2,1)} %add_convert_fusion.17), channel_id=1, source_target_pairs={{2,0},{3,1},{4,2},{5,3},{6,4},{7,5},{0,6},{1,7},{10,8},{11,9},{12,... | collective-permute-start | bytes 1179656 | tf_op jit(solution)/shard_map/ppermute | solution.py:23
  437.8 24.3 %psum.23 = f32[1536]{0:T(1024)} all-reduce(f32[1536]{0:T(1024)S(1)} %get-tuple-element.5), channel_id=1, replica_groups=mesh['row'=4,'col'=8] {'col'}, use_global_device_ids=true, to_apply=%region_7.8 | all-reduce | flops 1536 | bytes 12288 | tf_op jit(solution)/shard_map/psum | solution.py:122
  (255 shorter events, 202.0 us)
Async XLA Ops:
  0.6 90.8 %collective-permute-start.44 = (bf16[128,1536]{1,0:T(8,128)(2,1)}, bf16[128,1536]{1,0:T(8,128)(2,1)S(1)}, u32[]{:S(2)}, u32[]{:S(2)}) collective-permute-start(bf16[128,1536]{1,0:T(8,128)(2,1)} %param.9), channel_id=1, source_target_pairs={{4,0},{5,1},{6,2},{7,3},{0,4},{1,5},{2,6},{3,7},{12,8},{13,9},{14,... | collective-permute-start | bytes 1179656 | tf_op jit(solution)/shard_map/ppermute | solution.py:23
  17.4 83.9 %collective-permute-start.22 = (bf16[128,1536]{1,0:T(8,128)(2,1)S(1)}, bf16[128,1536]{1,0:T(8,128)(2,1)S(1)}, u32[]{:S(2)}, u32[]{:S(2)}) collective-permute-start(bf16[128,1536]{1,0:T(8,128)(2,1)S(1)} %get-tuple-element.43), channel_id=1, source_target_pairs={{6,0},{7,1},{0,2},{1,3},{2,4},{3,5},{4,6},{5,7},{14,8},{15,9},{8,1... | collective-permute-start | bytes 1179656 | tf_op jit(solution)/shard_map/ppermute | solution.py:23
  30.4 72.5 %collective-permute-start.14 = (bf16[128,1536]{1,0:T(8,128)(2,1)S(1)}, bf16[128,1536]{1,0:T(8,128)(2,1)S(1)}, u32[]{:S(2)}, u32[]{:S(2)}) collective-permute-start(bf16[128,1536]{1,0:T(8,128)(2,1)S(1)} %get-tuple-element.43), channel_id=1, source_target_pairs={{4,0},{5,1},{6,2},{7,3},{0,4},{1,5},{2,6},{3,7},{12,8},{13,9},{14,... | collective-permute-start | bytes 1179656 | tf_op jit(solution)/shard_map/ppermute | solution.py:23
  40.7 96.9 %collective-permute-start.31 = (bf16[128,3072]{1,0:T(8,128)(2,1)S(1)}, bf16[128,3072]{1,0:T(8,128)(2,1)S(1)}, u32[]{:S(2)}, u32[]{:S(2)}) collective-permute-start(bf16[128,3072]{1,0:T(8,128)(2,1)S(1)} %constant_dynamic-slice_fusion.7), channel_id=1, source_target_pairs={{8,0},{0,8},{24,16},{16,24},{9,1},{1,9},{25,17},{17,25},{10,2},{2,... | collective-permute-start | bytes 2359304 | tf_op jit(solution)/shard_map/ppermute | solution.py:23
  91.4 46.4 %collective-permute-start.1 = (bf16[128,3072]{1,0:T(8,128)(2,1)S(1)}, bf16[128,3072]{1,0:T(8,128)(2,1)S(1)}, u32[]{:S(2)}, u32[]{:S(2)}) collective-permute-start(bf16[128,3072]{1,0:T(8,128)(2,1)S(1)} %constant_dynamic-slice_fusion.15), channel_id=1, source_target_pairs={{8,0},{0,8},{24,16},{16,24},{9,1},{1,9},{25,17},{17,25},{10,2},{2,... | collective-permute-start | bytes 2359304 | tf_op jit(solution)/shard_map/ppermute | solution.py:23
  142.8 61.7 %collective-permute-start.39 = (bf16[64,3072]{1,0:T(8,128)(2,1)S(1)}, bf16[64,3072]{1,0:T(8,128)(2,1)S(1)}, u32[]{:S(2)}, u32[]{:S(2)}) collective-permute-start(bf16[64,3072]{1,0:T(8,128)(2,1)S(1)} %constant_dynamic-slice_fusion.4), channel_id=1, source_target_pairs={{16,0},{24,8},{0,16},{8,24},{17,1},{25,9},{1,17},{9,25},{18,2},{26... | collective-permute-start | bytes 1179656 | tf_op jit(solution)/shard_map/ppermute | solution.py:23
  150.9 45.2 %collective-permute-start.47 = (bf16[64,3072]{1,0:T(8,128)(2,1)S(1)}, bf16[64,3072]{1,0:T(8,128)(2,1)S(1)}, u32[]{:S(2)}, u32[]{:S(2)}) collective-permute-start(bf16[64,3072]{1,0:T(8,128)(2,1)S(1)} %constant_dynamic-slice_fusion.2), channel_id=1, source_target_pairs={{16,0},{24,8},{0,16},{8,24},{17,1},{25,9},{1,17},{9,25},{18,2},{26... | collective-permute-start | bytes 1179656 | tf_op jit(solution)/shard_map/ppermute | solution.py:23
  167.8 42.1 %collective-permute-start.9 = (bf16[64,3072]{1,0:T(8,128)(2,1)S(1)}, bf16[64,3072]{1,0:T(8,128)(2,1)S(1)}, u32[]{:S(2)}, u32[]{:S(2)}) collective-permute-start(bf16[64,3072]{1,0:T(8,128)(2,1)S(1)} %constant_dynamic-slice_fusion.12), channel_id=1, source_target_pairs={{16,0},{24,8},{0,16},{8,24},{17,1},{25,9},{1,17},{9,25},{18,2},{26... | collective-permute-start | bytes 1179656 | tf_op jit(solution)/shard_map/ppermute | solution.py:23
  204.5 39.1 %collective-permute-start.56 = (bf16[64,3072]{1,0:T(8,128)(2,1)S(1)}, bf16[64,3072]{1,0:T(8,128)(2,1)S(1)}, u32[]{:S(2)}, u32[]{:S(2)}) collective-permute-start(bf16[64,3072]{1,0:T(8,128)(2,1)S(1)} %get-tuple-element.51), channel_id=1, source_target_pairs={{16,0},{24,8},{0,16},{8,24},{17,1},{25,9},{1,17},{9,25},{18,2},{26... | collective-permute-start | bytes 1179656 | tf_op jit(solution)/shard_map/ppermute | solution.py:23
  209.9 42.1 %collective-permute-start.18 = (bf16[64,3072]{1,0:T(8,128)(2,1)S(1)}, bf16[64,3072]{1,0:T(8,128)(2,1)S(1)}, u32[]{:S(2)}, u32[]{:S(2)}) collective-permute-start(bf16[64,3072]{1,0:T(8,128)(2,1)S(1)} %multiply_convert_fusion.1), channel_id=1, source_target_pairs={{16,0},{24,8},{0,16},{8,24},{17,1},{25,9},{1,17},{9,25},{18,2},{26... | collective-permute-start | bytes 1179656 | tf_op jit(solution)/shard_map/ppermute | solution.py:23
  218.3 42.1 %collective-permute-start.48 = (bf16[64,3072]{1,0:T(8,128)(2,1)S(1)}, bf16[64,3072]{1,0:T(8,128)(2,1)S(1)}, u32[]{:S(2)}, u32[]{:S(2)}) collective-permute-start(bf16[64,3072]{1,0:T(8,128)(2,1)S(1)} %get-tuple-element.49), channel_id=1, source_target_pairs={{16,0},{24,8},{0,16},{8,24},{17,1},{25,9},{1,17},{9,25},{18,2},{26... | collective-permute-start | bytes 1179656 | tf_op jit(solution)/shard_map/ppermute | solution.py:23
  226.7 42.1 %collective-permute-start.10 = (bf16[64,3072]{1,0:T(8,128)(2,1)S(1)}, bf16[64,3072]{1,0:T(8,128)(2,1)S(1)}, u32[]{:S(2)}, u32[]{:S(2)}) collective-permute-start(bf16[64,3072]{1,0:T(8,128)(2,1)S(1)} %multiply_convert_fusion.2), channel_id=1, source_target_pairs={{16,0},{24,8},{0,16},{8,24},{17,1},{25,9},{1,17},{9,25},{18,2},{26... | collective-permute-start | bytes 1179656 | tf_op jit(solution)/shard_map/ppermute | solution.py:23
  235.2 41.7 %collective-permute-start.40 = (bf16[64,3072]{1,0:T(8,128)(2,1)S(1)}, bf16[64,3072]{1,0:T(8,128)(2,1)S(1)}, u32[]{:S(2)}, u32[]{:S(2)}) collective-permute-start(bf16[64,3072]{1,0:T(8,128)(2,1)S(1)} %get-tuple-element.47), channel_id=1, source_target_pairs={{16,0},{24,8},{0,16},{8,24},{17,1},{25,9},{1,17},{9,25},{18,2},{26... | collective-permute-start | bytes 1179656 | tf_op jit(solution)/shard_map/ppermute | solution.py:23
  260.5 77.1 %collective-permute-start.27 = (bf16[128,3072]{1,0:T(8,128)(2,1)S(1)}, bf16[128,3072]{1,0:T(8,128)(2,1)S(1)}, u32[]{:S(2)}, u32[]{:S(2)}) collective-permute-start(bf16[128,3072]{1,0:T(8,128)(2,1)S(1)} %pad_maximum_fusion.3), channel_id=1, source_target_pairs={{8,0},{0,8},{24,16},{16,24},{9,1},{1,9},{25,17},{17,25},{10,2},{2,... | collective-permute-start | bytes 2359304 | tf_op jit(solution)/shard_map/ppermute | solution.py:23
  268.9 44.4 %collective-permute-start.57 = (bf16[128,3072]{1,0:T(8,128)(2,1)S(1)}, bf16[128,3072]{1,0:T(8,128)(2,1)S(1)}, u32[]{:S(2)}, u32[]{:S(2)}) collective-permute-start(bf16[128,3072]{1,0:T(8,128)(2,1)S(1)} %pad_maximum_fusion.7), channel_id=1, source_target_pairs={{8,0},{0,8},{24,16},{16,24},{9,1},{1,9},{25,17},{17,25},{10,2},{2,... | collective-permute-start | bytes 2359304 | tf_op jit(solution)/shard_map/ppermute | solution.py:23
  276.9 55.7 %collective-permute-start.19 = (bf16[128,3072]{1,0:T(8,128)(2,1)S(1)}, bf16[128,3072]{1,0:T(8,128)(2,1)S(1)}, u32[]{:S(2)}, u32[]{:S(2)}) collective-permute-start(bf16[128,3072]{1,0:T(8,128)(2,1)S(1)} %pad_maximum_fusion.2), channel_id=1, source_target_pairs={{8,0},{0,8},{24,16},{16,24},{9,1},{1,9},{25,17},{17,25},{10,2},{2,... | collective-permute-start | bytes 2359304 | tf_op jit(solution)/shard_map/ppermute | solution.py:23
  304.0 100.2 %collective-permute-start.35 = (bf16[128,1536]{1,0:T(8,128)(2,1)S(1)}, bf16[128,1536]{1,0:T(8,128)(2,1)S(1)}, u32[]{:S(2)}, u32[]{:S(2)}) collective-permute-start(bf16[128,1536]{1,0:T(8,128)(2,1)S(1)} %split.73), channel_id=1, source_target_pairs={{1,0},{0,1},{3,2},{2,3},{5,4},{4,5},{7,6},{6,7},{9,8},{8,9},{11,10... | collective-permute-start | bytes 1179656 | tf_op jit(solution)/shard_map/ppermute | solution.py:23
  313.3 156.9 %collective-permute-start.5 = (bf16[128,1536]{1,0:T(8,128)(2,1)}, bf16[128,1536]{1,0:T(8,128)(2,1)S(1)}, u32[]{:S(2)}, u32[]{:S(2)}) collective-permute-start(bf16[128,1536]{1,0:T(8,128)(2,1)} %split.65), channel_id=1, source_target_pairs={{1,0},{0,1},{3,2},{2,3},{5,4},{4,5},{7,6},{6,7},{9,8},{8,9},{11,10... | collective-permute-start | bytes 1179656 | tf_op jit(solution)/shard_map/ppermute | solution.py:23
  323.4 53.3 %collective-permute-start.42 = (bf16[128,1536]{1,0:T(8,128)(2,1)S(1)}, bf16[128,1536]{1,0:T(8,128)(2,1)S(1)}, u32[]{:S(2)}, u32[]{:S(2)}) collective-permute-start(bf16[128,1536]{1,0:T(8,128)(2,1)S(1)} %split.75), channel_id=1, source_target_pairs={{1,0},{0,1},{3,2},{2,3},{5,4},{4,5},{7,6},{6,7},{9,8},{8,9},{11,10... | collective-permute-start | bytes 1179656 | tf_op jit(solution)/shard_map/ppermute | solution.py:23
  332.7 45.8 %collective-permute-start.50 = (bf16[128,1536]{1,0:T(8,128)(2,1)S(1)}, bf16[128,1536]{1,0:T(8,128)(2,1)S(1)}, u32[]{:S(2)}, u32[]{:S(2)}) collective-permute-start(bf16[128,1536]{1,0:T(8,128)(2,1)S(1)} %split.77), channel_id=1, source_target_pairs={{1,0},{0,1},{3,2},{2,3},{5,4},{4,5},{7,6},{6,7},{9,8},{8,9},{11,10... | collective-permute-start | bytes 1179656 | tf_op jit(solution)/shard_map/ppermute | solution.py:23
  337.6 41.6 %collective-permute-start.58 = (bf16[128,1536]{1,0:T(8,128)(2,1)S(1)}, bf16[128,1536]{1,0:T(8,128)(2,1)S(1)}, u32[]{:S(2)}, u32[]{:S(2)}) collective-permute-start(bf16[128,1536]{1,0:T(8,128)(2,1)S(1)} %split.79), channel_id=1, source_target_pairs={{1,0},{0,1},{3,2},{2,3},{5,4},{4,5},{7,6},{6,7},{9,8},{8,9},{11,10... | collective-permute-start | bytes 1179656 | tf_op jit(solution)/shard_map/ppermute | solution.py:23
  404.2 66.0 %collective-permute-start.13 = (bf16[128,1536]{1,0:T(8,128)(2,1)}, bf16[128,1536]{1,0:T(8,128)(2,1)S(1)}, u32[]{:S(2)}, u32[]{:S(2)}) collective-permute-start(bf16[128,1536]{1,0:T(8,128)(2,1)} %add_convert_fusion.19), channel_id=1, source_target_pairs={{6,0},{7,1},{0,2},{1,3},{2,4},{3,5},{4,6},{5,7},{14,8},{15,9},{8,1... | collective-permute-start | bytes 1179656 | tf_op jit(solution)/shard_map/ppermute | solution.py:23
  406.2 64.0 %collective-permute-start.21 = (bf16[128,1536]{1,0:T(8,128)(2,1)}, bf16[128,1536]{1,0:T(8,128)(2,1)S(1)}, u32[]{:S(2)}, u32[]{:S(2)}) collective-permute-start(bf16[128,1536]{1,0:T(8,128)(2,1)} %add_convert_fusion.18), channel_id=1, source_target_pairs={{4,0},{5,1},{6,2},{7,3},{0,4},{1,5},{2,6},{3,7},{12,8},{13,9},{14,... | collective-permute-start | bytes 1179656 | tf_op jit(solution)/shard_map/ppermute | solution.py:23
  418.4 51.9 %collective-permute-start.29 = (bf16[128,1536]{1,0:T(8,128)(2,1)}, bf16[128,1536]{1,0:T(8,128)(2,1)S(1)}, u32[]{:S(2)}, u32[]{:S(2)}) collective-permute-start(bf16[128,1536]{1,0:T(8,128)(2,1)} %add_convert_fusion.17), channel_id=1, source_target_pairs={{2,0},{3,1},{4,2},{5,3},{6,4},{7,5},{0,6},{1,7},{10,8},{11,9},{12,... | collective-permute-start | bytes 1179656 | tf_op jit(solution)/shard_map/ppermute | solution.py:23
  (52 other events, 1135.4 us)

commit v2 on v0

v2 whole, which is shorter than its diff:
```python
import functools

import jax
import jax.numpy as jnp
from jax import lax
from jax.experimental import pallas as pl
from jax.experimental.pallas import tpu as pltpu
from jax.sharding import PartitionSpec as P

MESH = pl.DeviceIdType.MESH
CORES = 2
LANES = 128
epsilon = 1e-06
ROOT_HALF = 0.7071067811865476
ROOT_TWO_PI = 0.3989422804014327
ROWS_ROWS = (((1,), (1,)), ((), ()))
ROWS_COLS = (((1,), (0,)), ((), ()))


def tile_of(size):
    return 512 if size % 512 == 0 else 256 if size % 256 == 0 else 128


def layer_kernel(
    rows, y_n, z_n, x_n,
    inputs, gain, weight_in, weight_out, cotangent,
    branch, input_gradient, gain_gradient, cot_all, scl_all, act_all, slo_all,
    w_in, w_out, part, core_in, y_in, own, lhs, x_in, z_in, scaled, stats, sums, gains,
    ag_s, ag_r, rc_s, rc_r, ry_s, ry_r, ay_s, ay_r, ac_s, ac_r, xs_s, xs_r, zs_s, zs_r,
    st_s, st_r, gn_s, gn_r, load, wload, keep,
):
    block, d = inputs.shape
    ff = w_in.shape[1]
    tokens = x_n * block
    half = tokens // CORES
    quarter = half // y_n
    cols = z_n * x_n
    width = d * rows
    row = lax.axis_index("row")
    col = lax.axis_index("col")
    y, core = row // CORES, row % CORES
    z, x = col // x_n, col % x_n

    def at_z(step):
        return (row, lax.rem(z + step + z_n, z_n) * x_n + x)

    def at_x(step):
        return (row, z * x_n + lax.rem(x + step + x_n, x_n))

    def at_y(step):
        return (lax.rem(y + step, y_n) * CORES + core, col)

    other_core = (y * CORES + 1 - core, col)

    def remote(src, dst, send, recv, device):
        return pltpu.make_async_remote_copy(
            src_ref=src, dst_ref=dst, send_sem=send, recv_sem=recv, device_id=device, device_id_type=MESH
        )

    def take(src, dst):
        copy = pltpu.make_async_copy(src, dst, load)
        copy.start()
        copy.wait()

    barrier = pltpu.get_barrier_semaphore()
    for step in range(1, rows):
        pl.semaphore_signal(barrier, inc=1, device_id=(lax.rem(row + step, rows), col), device_id_type=MESH)
    for step in range(1, cols):
        pl.semaphore_signal(barrier, inc=1, device_id=(row, lax.rem(col + step, cols)), device_id_type=MESH)
    weight_loads = [
        pltpu.make_async_copy(weight_out, w_out, wload.at[0]),
        pltpu.make_async_copy(weight_in, w_in, wload.at[1]),
    ]
    for copy in weight_loads:
        copy.start()
    pl.semaphore_wait(barrier, rows + cols - 2)

    gathered = (cot_all, scl_all)
    spread_out = (act_all, slo_all)

    def block_rows(dz, dx):
        return pl.ds(dz * tokens + dx * block, block)

    def z_send(a, dz, src):
        return remote(src, gathered[a].at[block_rows(dz, 0)], ag_s.at[a, dz, 0], ag_r.at[a, dz, 0], at_z(-dz))

    def x_send(a, dz, dx, src):
        return remote(src, gathered[a].at[block_rows(dz, dx)], ag_s.at[a, dz, dx], ag_r.at[a, dz, dx], at_x(-dx))

    def begin(a, src):
        for dx in range(1, x_n):
            x_send(a, 0, dx, src).start()
        if z_n > 1:
            z_send(a, 1, src).start()
        pltpu.make_async_copy(src, gathered[a].at[block_rows(0, 0)], keep.at[a]).start()

    def forward(a, dz, src):
        z_send(a, dz, src).wait_recv()
        for dx in range(1, x_n):
            x_send(a, dz, dx, gathered[a].at[block_rows(dz, 0)]).start()
        if dz + 1 < z_n:
            z_send(a, dz + 1, src).start()

    begin(0, cotangent)

    floats = inputs[...].astype(jnp.float32)
    lane = lax.broadcasted_iota(jnp.int32, (block, LANES), 1)

    def pair(first, second):
        return jnp.where(lane == 0, first, jnp.where(lane == 1, second, 0.0))

    def exchange(use):
        for step in range(1, rows):
            remote(
                stats.at[use, 0], stats.at[use, step], st_s.at[use, step], st_r.at[use, step],
                (lax.rem(row + step, rows), col),
            ).start()
        total = stats[use, 0]
        for step in range(1, rows):
            remote(
                stats.at[use, 0], stats.at[use, step], st_s.at[use, step], st_r.at[use, step],
                (lax.rem(row + step, rows), col),
            ).wait()
            total = total + stats[use, step]
        total = total / width
        return (
            jnp.sum(jnp.where(lane == 0, total, 0.0), axis=1, keepdims=True),
            jnp.sum(jnp.where(lane == 1, total, 0.0), axis=1, keepdims=True),
        )

    stats[0, 0] = pair(jnp.sum(floats, axis=1, keepdims=True), jnp.sum(floats * floats, axis=1, keepdims=True))
    center, meansq = exchange(0)
    spread = lax.rsqrt(meansq - center * center + epsilon)
    sums[0] = jnp.broadcast_to(center, (block, LANES))
    sums[1] = jnp.broadcast_to(spread, (block, LANES))
    scaled[...] = ((floats - center) * spread * gain[...]).astype(jnp.bfloat16)
    begin(1, scaled)

    def core_copy(a, g):
        return remote(
            part.at[a, g, pl.ds(pl.multiple_of((1 - core) * half, half), half)], core_in.at[a, g],
            rc_s.at[a, g], rc_r.at[a, g], other_core,
        )

    def y_copy(a, g, step):
        start = core * half + lax.rem(y + step, y_n) * quarter
        return remote(
            part.at[a, g, pl.ds(pl.multiple_of(start, quarter), quarter)], y_in.at[a, g, step - 1],
            ry_s.at[a, g, step], ry_r.at[a, g, step], at_y(step),
        )

    def multiply(right, dims, out_cols, store):
        tile = tile_of(out_cols)

        @pl.loop(0, out_cols // tile)
        def _(n):
            here = pl.ds(pl.multiple_of(n * tile, tile), tile)
            left = lhs[...] if store[2] == ff else lhs[:, :d]
            piece = right[here, :] if dims is ROWS_ROWS else right[:, here]
            value = lax.dot_general(left, piece, dims, preferred_element_type=jnp.float32).astype(jnp.bfloat16)
            a, g, _, offset = store
            part[a, g, :, pl.ds(pl.multiple_of(offset + n * tile, LANES), tile)] = value

    own_blocks = (cotangent, scaled)

    def project(a, g):
        if g == 0:
            pltpu.make_async_copy(own_blocks[a], gathered[a].at[block_rows(0, 0)], keep.at[a]).wait()
            weight_loads[a].wait()
        for dx in range(1, x_n):
            x_send(a, g, dx, own_blocks[a]).wait_recv()
        take(gathered[a].at[pl.ds(g * tokens, tokens)], lhs.at[:, pl.ds(0, d)])
        multiply(w_out if a == 0 else w_in, ROWS_ROWS if a == 0 else ROWS_COLS, ff, (a, g, d, 0))
        core_copy(a, g).start()

    def core_sum(a, g):
        core_copy(a, g).wait()
        mine = pl.ds(pl.multiple_of(core * half, half), half)
        tile = tile_of(ff)

        @pl.loop(0, ff // tile)
        def _(n):
            here = pl.ds(pl.multiple_of(n * tile, tile), tile)
            total = part[a, g, mine, here].astype(jnp.float32) + core_in[a, g, :, here].astype(jnp.float32)
            part[a, g, mine, here] = total.astype(jnp.bfloat16)

        for step in range(1, y_n):
            y_copy(a, g, step).start()

    def share_copy(a, g, step):
        start = g * tokens + core * half + y * quarter
        return remote(
            own.at[a, g], spread_out[a].at[pl.ds(pl.multiple_of(start, quarter), quarter)],
            ay_s.at[a, g, step], ay_r.at[a, g, step], at_y(step),
        )

    def share_keep(a, g):
        start = g * tokens + core * half + y * quarter
        return pltpu.make_async_copy(
            own.at[a, g], spread_out[a].at[pl.ds(pl.multiple_of(start, quarter), quarter)], ay_s.at[a, g, 0]
        )

    def activate(g):
        for a in range(2):
            for step in range(1, y_n):
                y_copy(a, g, step).wait()
        mine = pl.ds(pl.multiple_of(core * half + y * quarter, quarter), quarter)
        tile = tile_of(ff)

        @pl.loop(0, ff // tile)
        def _(n):
            here = pl.ds(pl.multiple_of(n * tile, tile), tile)
            back = part[0, g, mine, here].astype(jnp.float32)
            hidden = part[1, g, mine, here].astype(jnp.float32)
            for step in range(y_n - 1):
                back = back + y_in[0, g, step, :, here].astype(jnp.float32)
                hidden = hidden + y_in[1, g, step, :, here].astype(jnp.float32)
            cdf = 0.5 * (1.0 + lax.erf(hidden * ROOT_HALF))
            density = jnp.exp(-0.5 * hidden * hidden) * ROOT_TWO_PI
            own[0, g, :, here] = (hidden * cdf).astype(jnp.bfloat16)
            own[1, g, :, here] = (back * (cdf + hidden * density)).astype(jnp.bfloat16)

        for a in range(2):
            for step in range(1, y_n):
                share_copy(a, g, step).start()
            share_keep(a, g).start()

    def half_copy(a, g):
        here = pl.ds(pl.multiple_of(g * tokens + core * half, half), half)
        return remote(spread_out[a].at[here], spread_out[a].at[here], ac_s.at[a, g], ac_r.at[a, g], other_core)

    def pass_on(g):
        for a in range(2):
            for step in range(1, y_n):
                share_copy(a, g, step).wait()
            share_keep(a, g).wait()
            half_copy(a, g).start()

    def x_copy(a, g, dx):
        return remote(
            part.at[0, g, pl.ds(dx * block, block), pl.ds(a * d, d)], x_in.at[a, g, dx - 1],
            xs_s.at[a, g, dx], xs_r.at[a, g, dx], at_x(dx),
        )

    def z_copy(a, g):
        return remote(
            part.at[0, g, pl.ds(0, block), pl.ds(a * d, d)], z_in.at[a, g - 1], zs_s.at[a, g], zs_r.at[a, g], at_z(g)
        )

    def finish(a, g):
        half_copy(a, g).wait()
        take(spread_out[a].at[pl.ds(g * tokens, tokens)], lhs)
        multiply(w_out if a == 0 else w_in, ROWS_COLS if a == 0 else ROWS_ROWS, d, (0, g, ff, a * d))
        for dx in range(1, x_n):
            x_copy(a, g, dx).start()

    def x_sum(a, g):
        for dx in range(1, x_n):
            x_copy(a, g, dx).wait()
        if x_n > 1:
            total = part[0, g, :block, a * d : (a + 1) * d].astype(jnp.float32)
            for dx in range(1, x_n):
                total = total + x_in[a, g, dx - 1].astype(jnp.float32)
            part[0, g, :block, a * d : (a + 1) * d] = total.astype(jnp.bfloat16)
        if g:
            z_copy(a, g).start()

    for step in range(z_n + 4):
        for a in range(2):
            if step < z_n:
                project(a, step)
            if step + 1 < z_n:
                forward(a, step + 1, own_blocks[a])
        if step < z_n:
            for a in range(2):
                core_sum(a, step)
        if 0 <= step - 1 < z_n:
            activate(step - 1)
        if 0 <= step - 3 < z_n:
            for a in range(2):
                x_sum(a, step - 3)
        if 0 <= step - 2 < z_n:
            pass_on(step - 2)
            for a in range(2):
                finish(a, step - 2)

    def collected(a):
        total = part[0, 0, :block, a * d : (a + 1) * d].astype(jnp.float32)
        for g in range(1, z_n):
            z_copy(a, g).wait()
            total = total + z_in[a, g - 1].astype(jnp.float32)
        return total

    normed_gradient = collected(1)
    normed = (inputs[...].astype(jnp.float32) - sums[0][:, :1]) * sums[1][:, :1]
    gains[0] = jnp.broadcast_to(jnp.sum(normed_gradient * normed, axis=0, keepdims=True), gains.shape[1:])

    def gain_copy(step):
        return remote(gains.at[0], gains.at[step], gn_s.at[step], gn_r.at[step], (row, lax.rem(col + step, cols)))

    for step in range(1, cols):
        gain_copy(step).start()
    scaled_gradient = normed_gradient * gain[...]
    stats[1, 0] = pair(
        jnp.sum(scaled_gradient, axis=1, keepdims=True), jnp.sum(scaled_gradient * normed, axis=1, keepdims=True)
    )
    mean_gradient, mean_cross = exchange(1)
    input_gradient[...] = (sums[1][:, :1] * (scaled_gradient - mean_gradient - normed * mean_cross)).astype(jnp.bfloat16)
    branch[...] = collected(0).astype(jnp.bfloat16)
    total = gains[0]
    for step in range(1, cols):
        gain_copy(step).wait()
        total = total + gains[step]
    gain_gradient[...] = total
    for a in range(2):
        for dz in range(z_n):
            for dx in range(x_n):
                if dx:
                    x_send(a, dz, dx, own_blocks[a]).wait_send()
                elif dz:
                    z_send(a, dz, own_blocks[a]).wait_send()


def make_per_device(rows, cols):
    y_n = rows // CORES
    z_n = 4 if cols % 4 == 0 else 1
    x_n = cols // z_n

    def per_device(inputs, norm_gain, weight_in, weight_out, cotangent):
        block, d = inputs.shape
        ff = weight_in.shape[1]
        tokens = x_n * block
        half = tokens // CORES
        quarter = half // y_n
        every = z_n * tokens
        bf16, f32 = jnp.bfloat16, jnp.float32
        dma = pltpu.SemaphoreType.DMA
        vmem = pl.BlockSpec(memory_space=pltpu.VMEM)
        anywhere = pl.BlockSpec(memory_space=pl.ANY)

        def shape(*dims, dtype=bf16):
            return jax.ShapeDtypeStruct(dims, dtype)

        outs = pl.pallas_call(
            functools.partial(layer_kernel, rows, y_n, z_n, x_n),
            out_shape=(
                shape(block, d), shape(block, d), shape(8, d, dtype=f32),
                shape(every, d), shape(every, d), shape(every, ff), shape(every, ff),
            ),
            in_specs=[vmem, vmem, anywhere, anywhere, anywhere],
            out_specs=(vmem, vmem, vmem, anywhere, anywhere, anywhere, anywhere),
            scratch_shapes=[
                pltpu.VMEM((d, ff), bf16),
                pltpu.VMEM((ff, d), bf16),
                pltpu.VMEM((2, z_n, tokens, ff), bf16),
                pltpu.VMEM((2, z_n, half, ff), bf16),
                pltpu.VMEM((2, z_n, max(y_n - 1, 1), quarter, ff), bf16),
                pltpu.VMEM((2, z_n, quarter, ff), bf16),
                pltpu.VMEM((tokens, ff), bf16),
                pltpu.VMEM((2, z_n, max(x_n - 1, 1), block, d), bf16),
                pltpu.VMEM((2, max(z_n - 1, 1), block, d), bf16),
                pltpu.VMEM((block, d), bf16),
                pltpu.VMEM((2, rows, block, LANES), f32),
                pltpu.VMEM((2, block, LANES), f32),
                pltpu.VMEM((cols, 8, d), f32),
                dma((2, z_n, x_n)), dma((2, z_n, x_n)),
                dma((2, z_n)), dma((2, z_n)),
                dma((2, z_n, y_n)), dma((2, z_n, y_n)),
                dma((2, z_n, y_n)), dma((2, z_n, y_n)),
                dma((2, z_n)), dma((2, z_n)),
                dma((2, z_n, x_n)), dma((2, z_n, x_n)),
                dma((2, z_n)), dma((2, z_n)),
                dma((2, rows)), dma((2, rows)),
                dma((cols,)), dma((cols,)),
                dma, dma((2,)), dma((2,)),
            ],
            compiler_params=pltpu.CompilerParams(
                collective_id=0, has_side_effects=True, vmem_limit_bytes=62 * 1024 * 1024
            ),
            cost_estimate=pl.CostEstimate(
                flops=8 * every * d * ff, bytes_accessed=8 * d * ff, transcendentals=2 * every * ff // rows
            ),
        )(inputs, norm_gain[None, :], weight_in, weight_out, cotangent)
        branch, input_gradient, gain_gradient, cot_all, scl_all, act_all, slo_all = outs
        over_tokens = (((0,), (0,)), ((), ()))
        out_gradient = lax.dot_general(act_all, cot_all, over_tokens, preferred_element_type=f32)
        in_gradient = lax.dot_general(scl_all, slo_all, over_tokens, preferred_element_type=f32)
        return branch, input_gradient, in_gradient, out_gradient, gain_gradient[0]

    return per_device


def solution(mesh):
    in_specs = (P("col", "row"), P("row"), P("row", "col"), P("col", "row"), P("col", "row"))
    out_specs = (P("col", "row"), P("col", "row"), P("row", "col"), P("col", "row"), P("row"))
    per_device = make_per_device(mesh.shape["row"], mesh.shape["col"])
    return jax.shard_map(per_device, mesh=mesh, in_specs=in_specs, out_specs=out_specs, check_vma=False)
```

time: 531 us -> 286 us (0.54)
  waiting for transfers between devices: 365 us -> 0 us
  Pallas kernels: 0 us -> 250 us
  matrix products: 93.5 us -> 30.1 us
  blocking collectives: 35.8 us -> 0 us
  other arithmetic: 19.2 us -> 0 us
  between operations: 14.2 us -> 0.66 us
    pallas_call x0 -> x1, Pallas kernels: none -> 250 us  [per_device(): pl.pallas_call(functools.partial(layer_kernel, rows, y_n, z_n, x_n), out_...]
    all_gather x4 -> x0, waiting for transfers between devices: 182 us -> none  [the longest x1 60.1 us: per_device(): normed_all = lax.all_gather(scaled, 'col', axis=0, tiled=True)]
    reduce_scatter x4 -> x0, waiting for transfers between devices: 182 us -> none  [the longest x1 61.5 us: per_device(): lax.psum_scatter(lax.dot_general(cotangent_all, weight_out, (((1,), (1,))...]
    dot_general x6 -> x2, matrix products: 93.5 us -> 30.1 us  [the longest x1 17 us: per_device(): lax.dot_general(scl_all, slo_all, over_tokens, preferred_element_type=f32)]
    psum x3 -> x0, blocking collectives: 35.8 us -> none  [the longest x1 21.5 us: per_device(): gain_gradient = lax.psum(jnp.sum(normed_gradient * normed, axis=0), 'col')]
    convert_element_type x4 -> x0, other arithmetic: 16.6 us -> none  [the longest x1 9.39 us: per_device(): gelu_slope(hidden_part, active_part_gradient).astype(jnp.bfloat16)]
  transfers between devices with their start and end apart: 8 -> 0, of which waited for: 8 -> 0; matrix products, arithmetic and copies ran while one was open for 19% -> 0% of each run, Pallas kernels for 0% -> 0%
where the time goes in v2:
time: 286 us; the launch traced here: 285 us
  Pallas kernels  250 us (87%)
  matrix products  30.1 us (11%)
  local copies, waits for them, and re-layouts  4.22 us (1%)
    pallas_call x1, Pallas kernels, per_device(): pl.pallas_call(functools.partial(layer_kernel, rows, y_n, z_n, x_n), out_...  250 us
    dot_general x1, matrix products, per_device(): lax.dot_general(scl_all, slo_all, over_tokens, preferred_element_type=f32)  17 us
    dot_general x1, matrix products, per_device(): lax.dot_general(act_all, cot_all, over_tokens, preferred_element_type=f32)  13.2 us

profile of v2, /device:TPU:0, one launch (start us, length us, event | category | flops | bytes accessed | tf_op | source)
XLA Modules:
  0.0 284.7 jit_solution(15855308615886429423)
XLA Ops:
  0.6 1.3 broadcast_in_dim.3.gain
  1.9 249.7 %shard_map.92 = (bf16[128,1536]{1,0:T(8,128)(2,1)}, bf16[128,1536]{1,0:T(8,128)(2,1)}, f32[8,1536]{1,0:T(8,128)}, bf16[1024,1536]{1,0:T(8,128)(2,1)}, bf16[1024,...) custom-call(bf16[128,1536]{1,0:T(8,128)(2,1)} %inputs.1, ...), custom_call_target="tpu_custom_call" | custom-call | flops 38654705664 | bytes 37748736 | tf_op jit(solution)/shard_map/pallas_call | solution.py:344
  251.6 1.4 slice_reduce_fusion
  253.0 0.0 copy-start.2
  253.0 0.0 copy-start.3
  253.0 17.0 %fusion = f32[1536,3072]{1,0:T(8,128)} fusion(bf16[1024,1536]{1,0:T(8,128)(2,1)} %get-tuple-element.14, bf16[1024,3072]{1,0:T(8,128)(2,1)} %get-tuple-element.15), kind=kOutput, calls=%fused_computation.1 | convolution fusion | flops 9663676416 | bytes 28311552 | tf_op jit(solution)/shard_map/dot_general | solution.py:387
  270.0 0.0 copy-done.2
  270.0 0.0 copy-done.3
  270.0 0.0 copy-start.1
  270.0 0.0 copy-start
  270.0 13.2 %fusion.1 = f32[3072,1536]{1,0:T(8,128)} fusion(bf16[1024,3072]{1,0:T(8,128)(2,1)S(1)} %copy-done.2, bf16[1024,1536]{1,0:T(8,128)(2,1)S(1)} %copy-done.3), kind=kOutput, calls=%fused_computation.2 | convolution fusion | flops 9663676416 | bytes 28311552 | tf_op jit(solution)/shard_map/dot_general | solution.py:386
  283.2 0.0 copy-done.1
  283.2 0.7 copy.12
  283.9 0.0 copy-done
  283.9 0.7 copy.13
Async XLA Ops:
  253.0 17.0 %copy-start.2 = (bf16[1024,3072]{1,0:T(8,128)(2,1)S(1)}, bf16[1024,3072]{1,0:T(8,128)(2,1)}, u32[]{:S(2)}) copy-start(bf16[1024,3072]{1,0:T(8,128)(2,1)} %get-tuple-element.16) | copy-start | bytes 18874372
  253.0 17.0 %copy-start.3 = (bf16[1024,1536]{1,0:T(8,128)(2,1)S(1)}, bf16[1024,1536]{1,0:T(8,128)(2,1)}, u32[]{:S(2)}) copy-start(bf16[1024,1536]{1,0:T(8,128)(2,1)} %get-tuple-element.17) | copy-start | bytes 9437188
  270.0 13.2 %copy-start.1 = (bf16[128,1536]{1,0:T(8,128)(2,1)S(1)}, bf16[128,1536]{1,0:T(8,128)(2,1)}, u32[]{:S(2)}) copy-start(bf16[128,1536]{1,0:T(8,128)(2,1)} %get-tuple-element.24) | copy-start | bytes 1179652
  270.0 13.9 %copy-start = (bf16[128,1536]{1,0:T(8,128)(2,1)S(1)}, bf16[128,1536]{1,0:T(8,128)(2,1)}, u32[]{:S(2)}) copy-start(bf16[128,1536]{1,0:T(8,128)(2,1)} %get-tuple-element.25) | copy-start | bytes 1179652

commit v3 on v2

--- a/solution.py
+++ b/solution.py
@@ -220,21 +220,23 @@
             own[0, g, :, here] = (hidden * cdf).astype(jnp.bfloat16)
             own[1, g, :, here] = (back * (cdf + hidden * density)).astype(jnp.bfloat16)
 
+        for step in range(1, y_n):
+            share_copy(0, g, step).start()
         for a in range(2):
-            for step in range(1, y_n):
-                share_copy(a, g, step).start()
             share_keep(a, g).start()
 
     def half_copy(a, g):
         here = pl.ds(pl.multiple_of(g * tokens + core * half, half), half)
         return remote(spread_out[a].at[here], spread_out[a].at[here], ac_s.at[a, g], ac_r.at[a, g], other_core)
 
-    def pass_on(g):
-        for a in range(2):
+    def pass_on(a, g):
+        for step in range(1, y_n):
+            share_copy(a, g, step).wait()
+        if a == 0:
             for step in range(1, y_n):
-                share_copy(a, g, step).wait()
-            share_keep(a, g).wait()
-            half_copy(a, g).start()
+                share_copy(1, g, step).start()
+        share_keep(a, g).wait()
+        half_copy(a, g).start()
 
     def x_copy(a, g, dx):
         return remote(
@@ -265,24 +267,39 @@
         if g:
             z_copy(a, g).start()
 
-    for step in range(z_n + 4):
+    last = z_n - 1
+    for step in range(z_n + 3):
+        if step >= 2 and step - 2 < last:
+            pass_on(0, step - 2)
+        if step != 1 and step != 3 and 0 <= step - 1 < z_n:
+            activate(step - 1)
+        if 0 <= step - 3 < z_n:
+            pass_on(1, step - 3)
+            if step - 3 < last:
+                finish(0, step - 3)
+                if step - 3 == last - 1:
+                    pass_on(0, last)
+            finish(1, step - 3)
+        for a in range(2):
+            if 0 <= step - 4 < last - 1:
+                x_sum(a, step - 4)
+        if step == z_n + 1:
+            finish(0, last)
+            for a in range(2):
+                x_sum(a, last - 1)
         for a in range(2):
             if step < z_n:
                 project(a, step)
-            if step + 1 < z_n:
+                core_sum(a, step)
+                if step != 1 and step + 1 < z_n:
+                    forward(a, step + 1, own_blocks[a])
+        if step in (1, 3) and step - 1 < z_n:
+            activate(step - 1)
+        if step == 1 and step + 1 < z_n:
+            for a in range(2):
                 forward(a, step + 1, own_blocks[a])
-        if step < z_n:
-            for a in range(2):
-                core_sum(a, step)
-        if 0 <= step - 1 < z_n:
-            activate(step - 1)
-        if 0 <= step - 3 < z_n:
-            for a in range(2):
-                x_sum(a, step - 3)
-        if 0 <= step - 2 < z_n:
-            pass_on(step - 2)
-            for a in range(2):
-                finish(a, step - 2)
+    for a in range(2):
+        x_sum(a, last)
 
     def collected(a):
         total = part[0, 0, :block, a * d : (a + 1) * d].astype(jnp.float32)
@@ -293,7 +310,9 @@
 
     normed_gradient = collected(1)
     normed = (inputs[...].astype(jnp.float32) - sums[0][:, :1]) * sums[1][:, :1]
-    gains[0] = jnp.broadcast_to(jnp.sum(normed_gradient * normed, axis=0, keepdims=True), gains.shape[1:])
+    products = jnp.sum(normed_gradient * normed, axis=0, keepdims=True)
+    for n in range(d // LANES):
+        gains[0, n : n + 1, :] = products[:, n * LANES : (n + 1) * LANES]
 
     def gain_copy(step):
         return remote(gains.at[0], gains.at[step], gn_s.at[step], gn_r.at[step], (row, lax.rem(col + step, cols)))
@@ -344,7 +363,7 @@
         outs = pl.pallas_call(
             functools.partial(layer_kernel, rows, y_n, z_n, x_n),
             out_shape=(
-                shape(block, d), shape(block, d), shape(8, d, dtype=f32),
+                shape(block, d), shape(block, d), shape(d // LANES, LANES, dtype=f32),
                 shape(every, d), shape(every, d), shape(every, ff), shape(every, ff),
             ),
             in_specs=[vmem, vmem, anywhere, anywhere, anywhere],
@@ -362,7 +381,7 @@
                 pltpu.VMEM((block, d), bf16),
                 pltpu.VMEM((2, rows, block, LANES), f32),
                 pltpu.VMEM((2, block, LANES), f32),
-                pltpu.VMEM((cols, 8, d), f32),
+                pltpu.VMEM((cols, d // LANES, LANES), f32),
                 dma((2, z_n, x_n)), dma((2, z_n, x_n)),
                 dma((2, z_n)), dma((2, z_n)),
                 dma((2, z_n, y_n)), dma((2, z_n, y_n)),
@@ -385,7 +404,7 @@
         over_tokens = (((0,), (0,)), ((), ()))
         out_gradient = lax.dot_general(act_all, cot_all, over_tokens, preferred_element_type=f32)
         in_gradient = lax.dot_general(scl_all, slo_all, over_tokens, preferred_element_type=f32)
-        return branch, input_gradient, in_gradient, out_gradient, gain_gradient[0]
+        return branch, input_gradient, in_gradient, out_gradient, gain_gradient.reshape(-1)
 
     return per_device
 

time: 286 us -> 276 us (0.965)
  Pallas kernels: 250 us -> 241 us
    pallas_call x1, Pallas kernels: 250 us -> 241 us  [per_device(): pl.pallas_call(functools.partial(layer_kernel, rows, y_n, z_n, x_n), out_...]
where the time goes in v3:
time: 276 us; the launch traced here: 275 us
  Pallas kernels  241 us (87%)
  matrix products  30.4 us (11%)
  local copies, waits for them, and re-layouts  3.41 us (1%)
    pallas_call x1, Pallas kernels, per_device(): pl.pallas_call(functools.partial(layer_kernel, rows, y_n, z_n, x_n), out_...  241 us
    dot_general x1, matrix products, per_device(): lax.dot_general(scl_all, slo_all, over_tokens, preferred_element_type=f32)  17.2 us
    dot_general x1, matrix products, per_device(): lax.dot_general(act_all, cot_all, over_tokens, preferred_element_type=f32)  13.2 us

profile of v3, /device:TPU:0, one launch (start us, length us, event | category | flops | bytes accessed | tf_op | source)
XLA Modules:
  0.0 275.1 jit_solution(16606460194766367587)
XLA Ops:
  0.6 1.3 broadcast_in_dim.3.gain
  1.9 240.6 %shard_map.92 = (bf16[128,1536]{1,0:T(8,128)(2,1)}, bf16[128,1536]{1,0:T(8,128)(2,1)}, f32[12,128]{1,0:T(8,128)}, bf16[1024,1536]{1,0:T(8,128)(2,1)}, bf16[1024,...) custom-call(bf16[128,1536]{1,0:T(8,128)(2,1)} %inputs.1, ...), custom_call_target="tpu_custom_call" | custom-call | flops 38654705664 | bytes 37748736 | tf_op jit(solution)/shard_map/pallas_call | solution.py:363
  242.5 0.0 copy-start.3
  242.5 0.0 copy-start.4
  242.6 17.2 %fusion = f32[1536,3072]{1,0:T(8,128)} fusion(bf16[1024,1536]{1,0:T(8,128)(2,1)} %get-tuple-element.14, bf16[1024,3072]{1,0:T(8,128)(2,1)} %get-tuple-element.15), kind=kOutput, calls=%fused_computation | convolution fusion | flops 9663676416 | bytes 28311552 | tf_op jit(solution)/shard_map/dot_general | solution.py:406
  259.7 0.0 copy-done.3
  259.7 0.0 copy-done.4
  259.7 0.0 copy-start.1
  259.7 0.0 copy-start
  259.7 0.0 copy-start.2
  259.7 13.2 %fusion.1 = f32[3072,1536]{1,0:T(8,128)} fusion(bf16[1024,3072]{1,0:T(8,128)(2,1)S(1)} %copy-done.3, bf16[1024,1536]{1,0:T(8,128)(2,1)S(1)} %copy-done.4), kind=kOutput, calls=%fused_computation.1 | convolution fusion | flops 9663676416 | bytes 28311552 | tf_op jit(solution)/shard_map/dot_general | solution.py:405
  273.0 0.0 copy-done.1
  273.0 0.7 copy.13
  273.7 0.0 copy-done
  273.7 0.7 copy.14
  274.5 0.0 copy-done.2
  274.5 0.6 copy.15
Async XLA Ops:
  242.5 17.2 %copy-start.3 = (bf16[1024,3072]{1,0:T(8,128)(2,1)S(1)}, bf16[1024,3072]{1,0:T(8,128)(2,1)}, u32[]{:S(2)}) copy-start(bf16[1024,3072]{1,0:T(8,128)(2,1)} %get-tuple-element.16) | copy-start | bytes 18874372
  242.5 17.2 %copy-start.4 = (bf16[1024,1536]{1,0:T(8,128)(2,1)S(1)}, bf16[1024,1536]{1,0:T(8,128)(2,1)}, u32[]{:S(2)}) copy-start(bf16[1024,1536]{1,0:T(8,128)(2,1)} %get-tuple-element.17) | copy-start | bytes 9437188
  259.7 13.3 %copy-start.1 = (bf16[128,1536]{1,0:T(8,128)(2,1)S(1)}, bf16[128,1536]{1,0:T(8,128)(2,1)}, u32[]{:S(2)}) copy-start(bf16[128,1536]{1,0:T(8,128)(2,1)} %get-tuple-element.24) | copy-start | bytes 1179652
  259.7 14.0 %copy-start = (bf16[128,1536]{1,0:T(8,128)(2,1)S(1)}, bf16[128,1536]{1,0:T(8,128)(2,1)}, u32[]{:S(2)}) copy-start(bf16[128,1536]{1,0:T(8,128)(2,1)} %get-tuple-element.25) | copy-start | bytes 1179652
  259.7 14.7 %copy-start.2 = (f32[12,128]{1,0:T(8,128)S(1)}, f32[12,128]{1,0:T(8,128)}, u32[]{:S(2)}) copy-start(f32[12,128]{1,0:T(8,128)} %get-tuple-element.18) | copy-start | bytes 18436

commit v4 on v3

--- a/solution.py
+++ b/solution.py
@@ -19,6 +19,10 @@
 
 def tile_of(size):
     return 512 if size % 512 == 0 else 256 if size % 256 == 0 else 128
+
+
+def wide_tile_of(size):
+    return next((tile for tile in (1024, 768, 512, 256) if size % tile == 0), LANES)
 
 
 def layer_kernel(
@@ -57,11 +61,6 @@
             src_ref=src, dst_ref=dst, send_sem=send, recv_sem=recv, device_id=device, device_id_type=MESH
         )
 
-    def take(src, dst):
-        copy = pltpu.make_async_copy(src, dst, load)
-        copy.start()
-        copy.wait()
-
     barrier = pltpu.get_barrier_semaphore()
     for step in range(1, rows):
         pl.semaphore_signal(barrier, inc=1, device_id=(lax.rem(row + step, rows), col), device_id_type=MESH)
@@ -149,13 +148,13 @@
             ry_s.at[a, g, step], ry_r.at[a, g, step], at_y(step),
         )
 
-    def multiply(right, dims, out_cols, store):
-        tile = tile_of(out_cols)
+    def multiply(right, dims, out_cols, slot, store):
+        tile = wide_tile_of(out_cols)
 
         @pl.loop(0, out_cols // tile)
         def _(n):
             here = pl.ds(pl.multiple_of(n * tile, tile), tile)
-            left = lhs[...] if store[2] == ff else lhs[:, :d]
+            left = lhs[slot, :, : store[2]]
             piece = right[here, :] if dims is ROWS_ROWS else right[:, here]
             value = lax.dot_general(left, piece, dims, preferred_element_type=jnp.float32).astype(jnp.bfloat16)
             a, g, _, offset = store
@@ -163,14 +162,21 @@
 
     own_blocks = (cotangent, scaled)
 
+    def chunk_load(a, g):
+        return pltpu.make_async_copy(gathered[a].at[pl.ds(g * tokens, tokens)], lhs.at[a, :, pl.ds(0, d)], load.at[a])
+
+    def project_load(a, g):
+        if g == 0:
+            pltpu.make_async_copy(own_blocks[a], gathered[a].at[block_rows(0, 0)], keep.at[a]).wait()
+        for dx in range(1, x_n):
+            x_send(a, g, dx, own_blocks[a]).wait_recv()
+        chunk_load(a, g).start()
+
     def project(a, g):
         if g == 0:
-            pltpu.make_async_copy(own_blocks[a], gathered[a].at[block_rows(0, 0)], keep.at[a]).wait()
             weight_loads[a].wait()
-        for dx in range(1, x_n):
-            x_send(a, g, dx, own_blocks[a]).wait_recv()
-        take(gathered[a].at[pl.ds(g * tokens, tokens)], lhs.at[:, pl.ds(0, d)])
-        multiply(w_out if a == 0 else w_in, ROWS_ROWS if a == 0 else ROWS_COLS, ff, (a, g, d, 0))
+        chunk_load(a, g).wait()
+        multiply(w_out if a == 0 else w_in, ROWS_ROWS if a == 0 else ROWS_COLS, ff, a, (a, g, d, 0))
         core_copy(a, g).start()
 
     def core_sum(a, g):
@@ -249,10 +255,16 @@
             part.at[0, g, pl.ds(0, block), pl.ds(a * d, d)], z_in.at[a, g - 1], zs_s.at[a, g], zs_r.at[a, g], at_z(g)
         )
 
+    def finish_copy(a, g):
+        return pltpu.make_async_copy(spread_out[a].at[pl.ds(g * tokens, tokens)], lhs.at[a], load.at[a])
+
+    def finish_load(a, g):
+        half_copy(a, g).wait()
+        finish_copy(a, g).start()
+
     def finish(a, g):
-        half_copy(a, g).wait()
-        take(spread_out[a].at[pl.ds(g * tokens, tokens)], lhs)
-        multiply(w_out if a == 0 else w_in, ROWS_COLS if a == 0 else ROWS_ROWS, d, (0, g, ff, a * d))
+        finish_copy(a, g).wait()
+        multiply(w_out if a == 0 else w_in, ROWS_COLS if a == 0 else ROWS_ROWS, d, a, (0, g, ff, a * d))
         for dx in range(1, x_n):
             x_copy(a, g, dx).start()
 
@@ -268,38 +280,63 @@
             z_copy(a, g).start()
 
     last = z_n - 1
-    for step in range(z_n + 3):
-        if step >= 2 and step - 2 < last:
+
+    def both(action, g):
+        if 0 <= g < z_n:
+            for a in range(2):
+                action(a, g)
+
+    def project_both(g):
+        if g < z_n:
+            both(project_load, g)
+            if g >= 2:
+                forward_both(g + 1)
+            both(project, g)
+            both(core_sum, g)
+
+    def finish_both(g):
+        both(finish_load, g)
+        both(finish, g)
+
+    def forward_both(g):
+        if g < z_n:
+            for a in range(2):
+                forward(a, g, own_blocks[a])
+
+    for a in range(2):
+        project_load(a, 0)
+        project(a, 0)
+        if last:
+            forward(a, 1, own_blocks[a])
+    both(core_sum, 0)
+    for step in range(1, z_n + 1):
+        if step >= 2:
             pass_on(0, step - 2)
-        if step != 1 and step != 3 and 0 <= step - 1 < z_n:
+        if step == 2:
             activate(step - 1)
-        if 0 <= step - 3 < z_n:
+        project_both(step)
+        if step >= 3:
             pass_on(1, step - 3)
-            if step - 3 < last:
-                finish(0, step - 3)
-                if step - 3 == last - 1:
-                    pass_on(0, last)
-            finish(1, step - 3)
-        for a in range(2):
-            if 0 <= step - 4 < last - 1:
-                x_sum(a, step - 4)
-        if step == z_n + 1:
-            finish(0, last)
-            for a in range(2):
-                x_sum(a, last - 1)
-        for a in range(2):
-            if step < z_n:
-                project(a, step)
-                core_sum(a, step)
-                if step != 1 and step + 1 < z_n:
-                    forward(a, step + 1, own_blocks[a])
-        if step in (1, 3) and step - 1 < z_n:
+        if step != 2:
             activate(step - 1)
-        if step == 1 and step + 1 < z_n:
-            for a in range(2):
-                forward(a, step + 1, own_blocks[a])
-    for a in range(2):
-        x_sum(a, last)
+        if step == 1:
+            forward_both(2)
+        if step >= 3:
+            finish_both(step - 3)
+        both(x_sum, step - 4)
+    pass_on(0, last)
+    if last >= 1:
+        pass_on(1, last - 1)
+        both(x_sum, last - 2)
+        finish_both(last - 1)
+    finish_load(0, last)
+    finish(0, last)
+    both(x_sum, last - 1)
+    pass_on(1, last)
+    x_sum(0, last)
+    finish_load(1, last)
+    finish(1, last)
+    x_sum(1, last)
 
     def collected(a):
         total = part[0, 0, :block, a * d : (a + 1) * d].astype(jnp.float32)
@@ -375,7 +412,7 @@
                 pltpu.VMEM((2, z_n, half, ff), bf16),
                 pltpu.VMEM((2, z_n, max(y_n - 1, 1), quarter, ff), bf16),
                 pltpu.VMEM((2, z_n, quarter, ff), bf16),
-                pltpu.VMEM((tokens, ff), bf16),
+                pltpu.VMEM((2, tokens, ff), bf16),
                 pltpu.VMEM((2, z_n, max(x_n - 1, 1), block, d), bf16),
                 pltpu.VMEM((2, max(z_n - 1, 1), block, d), bf16),
                 pltpu.VMEM((block, d), bf16),
@@ -391,7 +428,7 @@
                 dma((2, z_n)), dma((2, z_n)),
                 dma((2, rows)), dma((2, rows)),
                 dma((cols,)), dma((cols,)),
-                dma, dma((2,)), dma((2,)),
+                dma((2,)), dma((2,)), dma((2,)),
             ],
             compiler_params=pltpu.CompilerParams(
                 collective_id=0, has_side_effects=True, vmem_limit_bytes=62 * 1024 * 1024

time: 276 us -> 279 us (1.011)
  Pallas kernels: 241 us -> 244 us
    pallas_call x1, Pallas kernels: 241 us -> 244 us  [per_device(): pl.pallas_call(functools.partial(layer_kernel, rows, y_n, z_n, x_n), out_...]
where the time goes in v4:
time: 279 us
  Pallas kernels  244 us (87%)
  matrix products  30.4 us (11%)
  local copies, waits for them, and re-layouts  3.41 us (1%)
    pallas_call x1, Pallas kernels, per_device(): pl.pallas_call(functools.partial(layer_kernel, rows, y_n, z_n, x_n), out_...  244 us
    dot_general x1, matrix products, per_device(): lax.dot_general(scl_all, slo_all, over_tokens, preferred_element_type=f32)  17 us
    dot_general x1, matrix products, per_device(): lax.dot_general(act_all, cot_all, over_tokens, preferred_element_type=f32)  13.5 us

profile of v4, /device:TPU:0, one launch (start us, length us, event | category | flops | bytes accessed | tf_op | source)
XLA Modules:
  0.0 279.0 jit_solution(16561687027042389804)
XLA Ops:
  0.6 1.3 broadcast_in_dim.3.gain
  1.9 244.5 %shard_map.92 = (bf16[128,1536]{1,0:T(8,128)(2,1)}, bf16[128,1536]{1,0:T(8,128)(2,1)}, f32[12,128]{1,0:T(8,128)}, bf16[1024,1536]{1,0:T(8,128)(2,1)}, bf16[1024,...) custom-call(bf16[128,1536]{1,0:T(8,128)(2,1)} %inputs.1, ...), custom_call_target="tpu_custom_call" | custom-call | flops 38654705664 | bytes 37748736 | tf_op jit(solution)/shard_map/pallas_call | solution.py:400
  246.4 0.0 copy-start.3
  246.4 0.0 copy-start.4
  246.4 17.0 %fusion = f32[1536,3072]{1,0:T(8,128)} fusion(bf16[1024,1536]{1,0:T(8,128)(2,1)} %get-tuple-element.14, bf16[1024,3072]{1,0:T(8,128)(2,1)} %get-tuple-element.15), kind=kOutput, calls=%fused_computation | convolution fusion | flops 9663676416 | bytes 28311552 | tf_op jit(solution)/shard_map/dot_general | solution.py:443
  263.4 0.0 copy-done.3
  263.4 0.0 copy-done.4
  263.4 0.0 copy-start.1
  263.4 0.0 copy-start
  263.4 0.0 copy-start.2
  263.4 13.5 %fusion.1 = f32[3072,1536]{1,0:T(8,128)} fusion(bf16[1024,3072]{1,0:T(8,128)(2,1)S(1)} %copy-done.3, bf16[1024,1536]{1,0:T(8,128)(2,1)S(1)} %copy-done.4), kind=kOutput, calls=%fused_computation.1 | convolution fusion | flops 9663676416 | bytes 28311552 | tf_op jit(solution)/shard_map/dot_general | solution.py:442
  276.9 0.0 copy-done.1
  276.9 0.7 copy.13
  277.6 0.0 copy-done
  277.6 0.7 copy.14
  278.4 0.0 copy-done.2
  278.4 0.6 copy.15
Async XLA Ops:
  246.4 17.0 %copy-start.3 = (bf16[1024,3072]{1,0:T(8,128)(2,1)S(1)}, bf16[1024,3072]{1,0:T(8,128)(2,1)}, u32[]{:S(2)}) copy-start(bf16[1024,3072]{1,0:T(8,128)(2,1)} %get-tuple-element.16) | copy-start | bytes 18874372
  246.4 17.0 %copy-start.4 = (bf16[1024,1536]{1,0:T(8,128)(2,1)S(1)}, bf16[1024,1536]{1,0:T(8,128)(2,1)}, u32[]{:S(2)}) copy-start(bf16[1024,1536]{1,0:T(8,128)(2,1)} %get-tuple-element.17) | copy-start | bytes 9437188
  263.4 13.5 %copy-start.1 = (bf16[128,1536]{1,0:T(8,128)(2,1)S(1)}, bf16[128,1536]{1,0:T(8,128)(2,1)}, u32[]{:S(2)}) copy-start(bf16[128,1536]{1,0:T(8,128)(2,1)} %get-tuple-element.24) | copy-start | bytes 1179652
  263.4 14.2 %copy-start = (bf16[128,1536]{1,0:T(8,128)(2,1)S(1)}, bf16[128,1536]{1,0:T(8,128)(2,1)}, u32[]{:S(2)}) copy-start(bf16[128,1536]{1,0:T(8,128)(2,1)} %get-tuple-element.25) | copy-start | bytes 1179652
  263.4 15.0 %copy-start.2 = (f32[12,128]{1,0:T(8,128)S(1)}, f32[12,128]{1,0:T(8,128)}, u32[]{:S(2)}) copy-start(f32[12,128]{1,0:T(8,128)} %get-tuple-element.18) | copy-start | bytes 18436
